TPU v7x, 32 devices: a whole 2x2x4 slice. The times are simulated.
32 devices in a mesh: seq: 16 (over z, y, x), tp: 2 (over core).
Axes of the slice: x: 2, y: 2, z: 4, core: 2. Of those that a mesh axis runs over, the one named last changes fastest.
Arguments:
- tokens: bfloat16 [2048, 2048], P(('seq', 'tp')), may hold values from -6 to 6
- block_ids: int32 [16, 2], replicated, may hold values from 0 to 31, as said below
- attn_gain: float32 [2048], replicated, may hold values from 0.25 to 1.75
- q_weight: bfloat16 [2048, 3072], P(None, 'tp'), may hold values from -0.125 to 0.125
- kv_weight: bfloat16 [2048, 576], replicated, may hold values from -0.125 to 0.125
- kv_gain: float32 [512], replicated, may hold values from 0.25 to 1.75
- uk_weight: bfloat16 [16, 512, 128], P('tp'), may hold values from -40 to 40
- uv_weight: bfloat16 [16, 512, 128], P('tp'), may hold values from -0.25 to 0.25
- o_weight: bfloat16 [2048, 2048], P('tp'), may hold values from -0.125 to 0.125
- ffn_gain: float32 [2048], replicated, may hold values from 0.25 to 1.75
- w_gate: bfloat16 [16, 2048, 1408], P('seq', None, 'tp'), may hold values from -0.125 to 0.125
- w_up: bfloat16 [16, 2048, 1408], P('seq', None, 'tp'), may hold values from -0.125 to 0.125
- w_down: bfloat16 [16, 1408, 2048], P('seq', 'tp'), may hold values from -0.15625 to 0.15625
- routes: int32 [2048, 6], P('seq'), may hold values from 0 to 15, all different within a row; in each aligned block of 64 rows (0 to 63, 64 to 127, ...) at most 36 rows name the same one
- gate_weights: float32 [2048, 6], P('seq'), may hold values from 0.1 to 1
Outputs:
- layer_out: bfloat16 [2048, 2048], P(('seq', 'tp'))
Inputs may be any that keep to these rules, and one draw needn't show every extreme that they name: `block_ids`: row d is (b, 31 - b) with b below 16; the first column names every b once. `routes`: each row names 6 different experts. In each aligned block of 64 rows (the tokens of one device) no expert is named by more than 36 rows, a bound that some block reaches.
All inputs are finite; a program needn't handle non-finite values.
Results may differ from a plain program's by a relative error of at most 0.027.
The roundings to bfloat16 on the way count: a program that leaves them out, or rounds other values in their place, can miss the bound.
Values may be sent and summed in bfloat16 or wider, within the bound.
No kernel may reach another device: no remote copies, remote signals or barrier semaphores. Data moves between devices by JAX's collectives and lax.ppermute only.
A program may use at most 128 MiB of HBM per device.

v0:
```python
import math

import jax
import jax.numpy as jnp
from jax import lax
from jax.sharding import PartitionSpec as P

EPSILON = 1e-06


def normalize(values, gain_vec):
    values = values.astype(jnp.float32)
    factor = lax.rsqrt(jnp.mean(values * values, axis=-1, keepdims=True) + EPSILON)
    return values * factor * gain_vec


def rotate(values, position):
    half_width = values.shape[-1] // 2
    frequency = jnp.exp(
        jnp.arange(half_width, dtype=jnp.float32) * (-2.0 * math.log(10000.0) / values.shape[-1])
    )
    angles = (
        position.astype(jnp.float32).reshape(position.shape + (1,) * (values.ndim - 1)) * frequency
    )
    cosine = jnp.cos(angles)
    sine_part = jnp.sin(angles)
    first_half = values[..., :half_width]
    second_half = values[..., half_width:]
    return jnp.concatenate(
        [
            first_half * cosine - second_half * sine_part,
            second_half * cosine + first_half * sine_part,
        ],
        axis=-1,
    )


def positions(row_ids, block_ids, rows_dev):
    half_width = rows_dev // 2
    device = row_ids // rows_dev
    within = row_ids % rows_dev
    block_num = block_ids.reshape(-1)[device * 2 + within // half_width]
    return block_num * half_width + within % half_width


def body(
    tokens,
    block_ids,
    attn_gain,
    q_weight,
    kv_weight,
    kv_gain,
    uk_weight,
    uv_weight,
    o_weight,
    ffn_gain,
    w_gate,
    w_up,
    w_down,
    routes,
    gate_weights,
):
    tp_count = lax.axis_size("tp")
    seq_count = lax.axis_size("seq")
    tp_index = lax.axis_index("tp")
    seq_index = lax.axis_index("seq")
    sub_rows = tokens.shape[0]
    dev_rows = sub_rows * tp_count
    model_dim = tokens.shape[1]
    head_count = uk_weight.shape[0]
    latent_dim = uk_weight.shape[1]
    nope_dim = uk_weight.shape[2]
    rope_dim = kv_weight.shape[1] - latent_dim
    value_dim = uv_weight.shape[2]
    top_count = routes.shape[1]
    capacity = min(sub_rows, max(2, 3 * sub_rows * top_count // (2 * seq_count)))
    score_scale = (nope_dim + rope_dim) ** (-0.5)
    all_tokens = lax.all_gather(tokens, "tp", axis=0, tiled=True)
    normed = normalize(all_tokens, attn_gain).astype(jnp.bfloat16)
    query_ids = seq_index * dev_rows + jnp.arange(dev_rows, dtype=jnp.int32)
    query_pos = positions(query_ids, block_ids, dev_rows)
    queries = jnp.dot(normed, q_weight, preferred_element_type=jnp.float32).astype(jnp.bfloat16)
    queries = queries.reshape(dev_rows, head_count, nope_dim + rope_dim)
    query_rope = rotate(queries[..., nope_dim:].astype(jnp.float32), query_pos).astype(jnp.bfloat16)
    query_latent = jnp.einsum(
        "thn,hln->thl", queries[..., :nope_dim], uk_weight, preferred_element_type=jnp.float32
    ).astype(jnp.bfloat16)
    projected = jnp.dot(normed, kv_weight, preferred_element_type=jnp.float32)
    latent = normalize(projected[:, :latent_dim], kv_gain).astype(jnp.bfloat16)
    key_rope = rotate(projected[:, latent_dim:], query_pos).astype(jnp.bfloat16)
    latent, key_rope = (latent, key_rope)
    run_max = jnp.full((dev_rows, head_count), -1e30, jnp.float32)
    piece_latent = lax.all_gather(latent, "seq", axis=0, tiled=True)
    piece_rope = lax.all_gather(key_rope, "seq", axis=0, tiled=True)
    count_rows = piece_latent.shape[0]
    key_pos = positions(jnp.arange(count_rows, dtype=jnp.int32), block_ids, dev_rows)
    scores = jnp.einsum(
        "thl,kl->thk", query_latent, piece_latent, preferred_element_type=jnp.float32
    )
    scores = scores + jnp.einsum(
        "thr,kr->thk", query_rope, piece_rope, preferred_element_type=jnp.float32
    )
    scores = scores * score_scale
    allowed = key_pos[None, None, :] <= query_pos[:, None, None]
    scores = jnp.where(allowed, scores, -1e30)
    new_max = jnp.maximum(run_max, jnp.max(scores, axis=-1))
    exp_terms = jnp.where(allowed, jnp.exp(scores - new_max[..., None]), 0.0)
    run_sum = jnp.sum(exp_terms, axis=-1)
    accumulated = jnp.einsum(
        "thk,kl->thl",
        exp_terms.astype(jnp.bfloat16),
        piece_latent,
        preferred_element_type=jnp.float32,
    )
    folded = (new_max, run_sum, accumulated)
    run_max, run_sum, accumulated = folded
    out_latent = (accumulated / run_sum[..., None]).astype(jnp.bfloat16)
    head_out = jnp.einsum(
        "thl,hlv->thv", out_latent, uv_weight, preferred_element_type=jnp.float32
    ).astype(jnp.bfloat16)
    partial_out = jnp.dot(
        head_out.reshape(dev_rows, head_count * value_dim),
        o_weight,
        preferred_element_type=jnp.float32,
    )
    expert_ids = jnp.arange(seq_count, dtype=jnp.int32)

    def slot_table(route_rows):
        flat_ids = route_rows.reshape(-1)
        onehot = (flat_ids[:, None] == expert_ids[None, :]).astype(jnp.int32)
        rank_table = jnp.cumsum(onehot, axis=0) - onehot
        return flat_ids * capacity + jnp.sum(rank_table * onehot, axis=1)

    own_routes = lax.dynamic_slice_in_dim(routes, tp_index * sub_rows, sub_rows, 0)
    own_weights = lax.dynamic_slice_in_dim(gate_weights, tp_index * sub_rows, sub_rows, 0)
    attn_own = lax.psum_scatter(
        partial_out.astype(jnp.bfloat16), "tp", scatter_dimension=0, tiled=True
    ).astype(jnp.float32)
    mixed_rows = (tokens.astype(jnp.float32) + attn_own).astype(jnp.bfloat16)
    normed_own = normalize(mixed_rows, ffn_gain).astype(jnp.bfloat16)
    target = slot_table(own_routes)
    source = jnp.arange(target.shape[0], dtype=jnp.int32) // top_count
    buffer = (
        jnp.zeros((seq_count * capacity, model_dim), jnp.bfloat16)
        .at[target]
        .set(normed_own[source])
    )
    packed = buffer.reshape(seq_count, capacity, model_dim)
    arrived = lax.all_to_all(packed, "seq", split_axis=0, concat_axis=0, tiled=True)
    piece_data = lax.all_gather(arrived, "tp", axis=0, tiled=True)
    flat_rows = piece_data.reshape(-1, model_dim)
    gate_part = jnp.dot(flat_rows, w_gate[0], preferred_element_type=jnp.float32)
    up_part = jnp.dot(flat_rows, w_up[0], preferred_element_type=jnp.float32)
    hidden = (
        (jax.nn.silu(gate_part) * up_part)
        .astype(jnp.bfloat16)
        .reshape(piece_data.shape[0], capacity, -1)
        .reshape(-1, w_up.shape[2])
    )
    down_local = w_down[0]
    expert_out = lax.psum_scatter(
        jnp.dot(hidden, down_local, preferred_element_type=jnp.float32).astype(jnp.bfloat16),
        "tp",
        scatter_dimension=0,
        tiled=True,
    ).astype(jnp.float32)
    expert_out = expert_out.astype(jnp.bfloat16).reshape(seq_count, capacity, model_dim)
    returned = lax.all_to_all(expert_out, "seq", split_axis=0, concat_axis=0, tiled=True).reshape(
        seq_count * capacity, model_dim
    )
    picked = (
        returned[slot_table(own_routes)].astype(jnp.float32).reshape(sub_rows, top_count, model_dim)
    )
    combined = jnp.sum(picked * own_weights[..., None], axis=1)
    return (mixed_rows.astype(jnp.float32) + combined).astype(jnp.bfloat16)


def solution(mesh):
    return jax.shard_map(
        body,
        mesh=mesh,
        in_specs=(
            P(("seq", "tp"), None),
            P(),
            P(),
            P(None, "tp"),
            P(),
            P(),
            P("tp", None, None),
            P("tp", None, None),
            P("tp", None),
            P(),
            P("seq", None, "tp"),
            P("seq", None, "tp"),
            P("seq", "tp", None),
            P("seq", None),
            P("seq", None),
        ),
        out_specs=P(("seq", "tp"), None),
        check_vma=False,
    )
```

profile of v0, /device:TPU:14, one launch (start us, length us, event | category | flops | bytes accessed | tf_op | source)
XLA Modules:
  0.0 366.9 jit_solution(1029727295614620031)
XLA Ops:
  6.5 2.5 all_gather.12
  9.1 0.2 fusion.19
  9.3 2.5 fusion.37
  11.9 0.6 copy-done.4
  12.5 0.8 multiply_convert_fusion
  13.4 4.6 %convolution_convert_fusion.2 = bf16[128,1536]{1,0:T(8,128)(2,1)} fusion(bf16[2048,1536]{1,0:T(8,128)(2,1)} %param.18, bf16[128,2048]{1,0:T(8,128)(2,1)S(1)} %all_gather.12, f32[2048]{0:T(1024)S(1)} %copy-done.6, f32[128]{0:T(128)S(1)} %add_rsqrt_fusion.2), kind=kOutput, calls=%fused_computation.21 | convolution fusion | flops 806551552 | bytes 7217664 | tf_op jit(solution)/shard_map/dot_general | solution.py:82
  18.0 1.9 copy.31
  20.1 1.2 gather_fusion
  21.4 0.1 compare_reduce_fusion
  21.6 0.1 compare_reduce_fusion.2
  21.7 0.1 compare_reduce_fusion.3
  21.7 0.1 compare_reduce_fusion.4
  21.8 0.1 compare_reduce_fusion.5
  21.9 0.1 compare_reduce_fusion.6
  22.0 0.1 compare_reduce_fusion.7
  22.5 0.1 compare_reduce_fusion.12
  22.6 0.1 compare_reduce_fusion.13
  22.7 0.1 compare_reduce_fusion.14
  23.7 0.9 multiply_cosine_fusion
  24.6 0.7 fusion.66
  25.3 0.7 fusion.65
  26.1 31.8 %all_gather.14 = bf16[2048,64]{0,1:T(8,128)(2,1)S(1)} all-gather(bf16[128,64]{0,1:T(8,128)(2,1)S(1)} %pad_maximum_fusion), channel_id=1, replica_groups=mesh['seq'=16,'tp'=2] {'seq'}, dimensions={0}, use_global_device_ids=true | all-gather | bytes 278528 | tf_op jit(solution)/shard_map/all_gather | solution.py:94
  57.9 4.4 %compare_select_fusion.1 = s32[2048,1]{0,1:T(1,128)S(1)} fusion(s32[]{:T(128)} %bitcast.25, s32[]{:T(128)} %bitcast.26, s32[]{:T(128)} %bitcast.27, s32[]{:T(128)} %bitcast.28, s32[]{:T(128)} %bitcast.29, s32[]{:T(128)} %bitcast.31, s32[]{:T(128)} %bitcast.30), kind=kLoop, calls=%fused_computation.83 | loop fusion | flops 90112 | bytes 8220 | tf_op jit(solution)/shard_map/gather | solution.py:42
  62.3 15.7 %fusion.48 = s32[2048]{0:T(1024)S(1)} fusion(pred[2048]{0:T(1024)(128)(4,1)S(1)} %compare_reduce_fusion, pred[2048]{0:T(1024)(128)(4,1)S(1)} %compare_reduce_fusion.1, pred[2048]{0:T(1024)(128)(4,1)S(1)} %compare_reduce_fusion.2, pred[2048]{0:T(1024)(128)(4,1)S(1)} %compare_reduce_fusion.3, pred[2048]{0:T(1024)(128)(4,1)S(1)} %compare_reduce_fusion.4, ...), kind=kLoop, calls=%fused_computation.119 | loop fusion | flops 90112 | bytes 67684 | tf_op jit(solution)/shard_map/add | solution.py:43
  78.0 0.9 slice_convert_fusion
  79.0 0.2 broadcast_compare_fusion
  79.2 7.9 %fusion.13 = f32[128,8,2048]{2,0,1:T(8,128)} fusion(bf16[2048,512]{0,1:T(8,128)(2,1)} %all-gather.3.cloned.1.call-done, bf16[8,512,128]{2,1,0:T(8,128)(2,1)} %param.21, bf16[128,8,192]{0,2,1:T(8,128)(2,1)} %bitcast.97), kind=kOutput, calls=%fused_computation.23 | convolution fusion | flops 2282225664 | bytes 11796480 | tf_op jit(solution)/shard_map/thl,kl->thk/dot_general | solution.py:97
  87.1 5.4 %fusion.67 = (f32[128,8]{0,1:T(8,128)S(1)}, f32[128,8,2048]{2,0,1:T(8,128)S(1)}) fusion(f32[128,8,2048]{2,0,1:T(8,128)} %fusion.13, bf16[2048,64]{0,1:T(8,128)(2,1)S(1)} %all_gather.14, bf16[128,8,32]{0,2,1:T(8,128)(2,1)S(1)} %get-tuple-element.12, bf16[128,8,32]{0,2,1:T(8,128)(2,1)S(1)} %get-tuple-element.11, pred[128,2048]{1,0:T(8,128)(4,1)S(1)} %broadcast_compare_fusion), kind=kOutput, calls=%fused_computation.169 | convolution fusion | flops 277085184 | bytes 17436672 | tf_op jit(solution)/shard_map/thr,kr->thk/dot_general | solution.py:100
  92.5 3.2 copy-done.1
  95.8 2.0 fusion
  97.8 7.0 %convolution_convert_fusion.4 = bf16[8,128,128]{1,2,0:T(8,128)(2,1)S(1)} fusion(bf16[8,512,128]{2,1,0:T(8,128)(2,1)} %param.22, f32[128,8]{0,1:T(8,128)S(1)} %fusion, f32[128,8,2048]{2,0,1:T(8,128)} %copy-done.1, f32[128,8]{0,1:T(8,128)S(1)} %broadcast_maximum_fusion, pred[128,2048]{1,0:T(8,128)(4,1)S(1)} %broadcast_compare_fusion, ...), kind=kOutput, calls=%fused_computation.32 | convolution fusion | flops 2289172480 | bytes 12066816 | tf_op jit(solution)/shard_map/thl,hlv->thv/dot_general | solution.py:118
  104.8 3.8 %convolution_convert_fusion.1 = bf16[128,2048]{1,0:T(8,128)(2,1)} fusion(bf16[128,1024]{0,1:T(8,128)(2,1)S(1)} %bitcast.98, bf16[1024,2048]{1,0:T(8,128)(2,1)} %param.23), kind=kOutput, calls=%fused_computation.20 | convolution fusion | flops 537133056 | bytes 4980736 | tf_op jit(solution)/shard_map/dot_general | solution.py:121
  108.5 0.3 all-gather.5.cloned.1.call-start
  108.9 0.1 copy.37
  109.0 0.1 eq.38
  109.1 0.1 eq.42
  109.3 0.1 copy.36
  109.4 0.1 mul.267
  109.5 0.9 reduce-window.6
  110.4 0.2 slice_reduce_fusion
  110.8 13.6 %reduce-scatter.3.cloned.1.call-done = bf16[64,2048]{1,0:T(8,128)(2,1)} async-done(((bf16[128,2048]{1,0:T(8,128)(2,1)}), bf16[64,2048]{1,0:T(8,128)(2,1)}) %reduce-scatter.3.cloned.1.call-update) | async-done | bytes 262160 | tf_op jit(solution)/shard_map/reduce_scatter | solution.py:136
  124.5 1.1 fusion.30
  125.6 1.1 fusion.32
  126.7 9.5 %scatter_custom_fusion = bf16[576,2048]{1,0:T(8,128)(2,1)} fusion(s32[384]{0:T(512)S(1)} %fusion.54, bf16[64,2048]{1,0:T(8,128)(2,1)S(1)} %fusion.32, s32[1024]{0:T(1024)S(1)} %pad_clamp_fusion.1, bf16[]{:T(256)} %constant.147.clone.1), kind=kCustom, calls=%fused_computation.26 | custom fusion | bytes 2359298 | tf_op jit(solution)/shard_map/scatter | solution.py:146
  136.2 4.1 %reshape.569 = bf16[16,36,2048]{2,1,0:T(8,128)(2,1)} reshape(bf16[576,2048]{1,0:T(8,128)(2,1)} %scatter_custom_fusion) | data formatting | bytes 4718592 | tf_op jit(solution)/shard_map/reshape | solution.py:148
  140.3 65.4 %all_to_all.10 = bf16[16,36,2048]{2,1,0:T(8,128)(2,1)S(1)} all-to-all(bf16[16,36,2048]{2,1,0:T(8,128)(2,1)} %reshape.569), channel_id=1, replica_groups=mesh['seq'=16,'tp'=2] {'seq'}, dimensions={0} | all-to-all | bytes 4718592 | tf_op jit(solution)/shard_map/all_to_all | solution.py:149
  205.7 2.7 copy.40
  208.4 0.3 reduce-scatter.5.cloned.1.call-start
  208.7 14.5 %all-gather.5.cloned.1.call-done = bf16[32,36,2048]{2,0,1:T(8,128)(2,1)} async-done(((bf16[16,36,2048]{2,0,1:T(8,128)(2,1)}), bf16[32,36,2048]{2,0,1:T(8,128)(2,1)}) %all-gather.5.cloned.1.call-update) | async-done | bytes 4718608 | tf_op jit(solution)/shard_map/all_gather | solution.py:150
  223.3 7.3 %copy.41 = bf16[32,36,2048]{2,1,0:T(8,128)(2,1)} copy(bf16[32,36,2048]{2,0,1:T(8,128)(2,1)} %all-gather.5.cloned.1.call-done) | data formatting | bytes 9437184 | tf_op jit(solution)/shard_map/all_gather | solution.py:150
  230.5 7.2 %reshape.570 = bf16[1152,2048]{1,0:T(8,128)(2,1)} reshape(bf16[32,36,2048]{2,1,0:T(8,128)(2,1)} %copy.41) | data formatting | bytes 9437184 | tf_op jit(solution)/shard_map/reshape | solution.py:151
  237.8 7.3 %fusion.10 = f32[1152,704]{0,1:T(8,128)S(1)} fusion(bf16[1152,2048]{1,0:T(8,128)(2,1)} %reshape.570, bf16[1,2048,704]{1,2,0:T(8,128)(2,1)} %param.25), kind=kOutput, calls=%fused_computation.18 | convolution fusion | flops 3321888768 | bytes 10846208 | tf_op jit(solution)/shard_map/dot_general | solution.py:152
  245.1 4.0 %fusion.7 = bf16[1152,704]{0,1:T(8,128)(2,1)S(1)} fusion(bf16[1152,2048]{1,0:T(8,128)(2,1)S(1)} %copy-done.2, f32[1152,704]{0,1:T(8,128)S(1)} %fusion.10, bf16[1,2048,704]{1,2,0:T(8,128)(2,1)S(1)} %copy-done.12), kind=kOutput, calls=%fused_computation.15 | convolution fusion | flops 3326754816 | bytes 12468224 | tf_op jit(solution)/shard_map/dot_general | solution.py:153
  249.1 5.6 %convolution_convert_fusion = bf16[1152,2048]{1,0:T(8,128)(2,1)} fusion(bf16[1152,704]{0,1:T(8,128)(2,1)S(1)} %fusion.7, bf16[1,704,2048]{2,1,0:T(8,128)(2,1)S(1)} %copy-done), kind=kOutput, calls=%fused_computation.6 | convolution fusion | flops 3324248064 | bytes 9224192 | tf_op jit(solution)/shard_map/dot_general | solution.py:162
  254.7 13.9 %reduce-scatter.5.cloned.1.call-done = bf16[576,2048]{1,0:T(8,128)(2,1)} async-done(((bf16[1152,2048]{1,0:T(8,128)(2,1)}), bf16[576,2048]{1,0:T(8,128)(2,1)}) %reduce-scatter.5.cloned.1.call-update) | async-done | bytes 2359312 | tf_op jit(solution)/shard_map/reduce_scatter | solution.py:161
  268.6 4.1 %reshape.571 = bf16[16,36,2048]{2,1,0:T(8,128)(2,1)} reshape(bf16[576,2048]{1,0:T(8,128)(2,1)} %reduce-scatter.5.cloned.1.call-done) | data formatting | bytes 4718592 | tf_op jit(solution)/shard_map/reshape | solution.py:167
  272.7 7.5 %all-to-all-start.1 = ((bf16[16,36,2048]{2,1,0:T(8,128)(2,1)}), bf16[16,36,2048]{2,1,0:T(8,128)(2,1)}, u32[]{:S(2)}, u32[]{:S(2)}) async-start(bf16[16,36,2048]{2,1,0:T(8,128)(2,1)} %reshape.571), calls=%async_computation.3 | async-start | bytes 5242880 | tf_op jit(solution)/shard_map/all_to_all | solution.py:168
  280.3 0.1 copy.42
  280.4 59.8 %all-to-all-done.1 = bf16[16,36,2048]{2,1,0:T(8,128)(2,1)} async-done(((bf16[16,36,2048]{2,1,0:T(8,128)(2,1)}), bf16[16,36,2048]{2,1,0:T(8,128)(2,1)}, u32[]{:S(2)}, u32[]{:S(2)}) %all-to-all-start.1) | async-done | bytes 2359328 | tf_op jit(solution)/shard_map/all_to_all | solution.py:168
  340.2 4.1 %reshape.572 = bf16[576,2048]{1,0:T(8,128)(2,1)} reshape(bf16[16,36,2048]{2,1,0:T(8,128)(2,1)} %all-to-all-done.1) | data formatting | bytes 4718592 | tf_op jit(solution)/shard_map/reshape | solution.py:168
  344.3 7.0 %gather_fusion.1 = bf16[384,2048]{1,0:T(8,128)(2,1)} fusion(bf16[576,2048]{1,0:T(8,128)(2,1)} %reshape.572, s32[1024]{0:T(1024)S(1)} %pad_clamp_fusion), kind=kCustom, calls=%fused_computation.2 | custom fusion | bytes 3147264 | tf_op jit(solution)/shard_map/gather | solution.py:172
  351.3 3.9 %reshape.573 = f32[64,6,2048]{2,1,0:T(8,128)} reshape(bf16[384,2048]{1,0:T(8,128)(2,1)} %gather_fusion.1) | data formatting | bytes 4718592 | tf_op jit(solution)/shard_map/convert_element_type | solution.py:172
  355.2 3.8 %multiply_reduce_fusion = f32[64,2048]{1,0:T(8,128)S(1)} fusion(f32[64,6,2048]{2,1,0:T(8,128)} %reshape.573, f32[64,6]{1,0:T(8,128)S(1)} %copy.42), kind=kLoop, calls=%fused_computation.10 | loop fusion | flops 1441792 | bytes 3671552 | tf_op jit(solution)/shard_map/reduce_sum | solution.py:174
  359.0 0.8 fusion.33
  (68 shorter events, 2.3 us)
Async XLA Ops:
  6.5 242.6 %copy-start = (bf16[1,704,2048]{2,1,0:T(8,128)(2,1)S(1)}, bf16[1,704,2048]{2,1,0:T(8,128)(2,1)}, u32[]{:S(2)}) copy-start(bf16[1,704,2048]{2,1,0:T(8,128)(2,1)} %param.27) | copy-start | bytes 8650756
  6.5 6.9 %copy-start.6 = (f32[2048]{0:T(1024)S(1)}, f32[2048]{0:T(1024)}, u32[]{:S(2)}) copy-start(f32[2048]{0:T(1024)} %param.17) | copy-start | bytes 24580
  6.5 6.0 %copy-start.10 = (f32[512]{0:T(512)S(1)}, f32[512]{0:T(512)}, u32[]{:S(2)}) copy-start(f32[512]{0:T(512)} %param.20) | copy-start | bytes 6148
  6.5 72.7 %all-gather.3.cloned.1.call-start = ((), (), s32[]{:S(2)}) async-start(), calls=%async_computation.4 | async-start | bytes 2228224 | tf_op jit(solution)/shard_map/all_gather | solution.py:93
  11.8 0.7 copy-start.4
  13.3 111.1 %reduce-scatter.3.cloned.1.call-start = ((), (), s32[]{:S(2)}) async-start(), calls=%async_computation.5 | async-start | bytes 786432 | tf_op jit(solution)/shard_map/reduce_scatter | solution.py:136
  13.4 6.5 %copy-start.11 = (s32[16,2]{0,1:T(2,128)S(1)}, s32[16,2]{0,1:T(2,128)}, u32[]{:S(2)}) copy-start(s32[16,2]{0,1:T(2,128)} %param.16) | copy-start | bytes 388
  92.5 3.2 copy-start.1
  104.7 4.1 %copy-start.8 = (s32[128,6]{0,1:T(8,128)S(1)}, s32[128,6]{0,1:T(8,128)}, u32[]{:S(2)}) copy-start(s32[128,6]{0,1:T(8,128)} %param.28) | copy-start | bytes 9220
  104.7 19.7 %copy-start.3 = (bf16[64,2048]{1,0:T(8,128)(2,1)S(1)}, bf16[64,2048]{1,0:T(8,128)(2,1)}, u32[]{:S(2)}) copy-start(bf16[64,2048]{1,0:T(8,128)(2,1)} %param.15) | copy-start | bytes 786436
  104.8 20.9 %copy-start.7 = (f32[2048]{0:T(1024)S(1)}, f32[2048]{0:T(1024)}, u32[]{:S(2)}) copy-start(f32[2048]{0:T(1024)} %param.24) | copy-start | bytes 24580
  108.5 114.7 %all-gather.5.cloned.1.call-start = ((), (), s32[]{:S(2)}) async-start(), calls=%async_computation.6 | async-start | bytes 7077888 | tf_op jit(solution)/shard_map/all_gather | solution.py:150
  208.4 60.1 %reduce-scatter.5.cloned.1.call-start = ((), (), s32[]{:S(2)}) async-start(), calls=%async_computation.7 | async-start | bytes 7077888 | tf_op jit(solution)/shard_map/reduce_scatter | solution.py:161
  237.8 7.3 %copy-start.2 = (bf16[1152,2048]{1,0:T(8,128)(2,1)S(1)}, bf16[1152,2048]{1,0:T(8,128)(2,1)}, u32[]{:S(2)}) copy-start(bf16[1152,2048]{1,0:T(8,128)(2,1)} %reshape.570) | copy-start | bytes 14155780
  237.8 7.3 %copy-start.12 = (bf16[1,2048,704]{1,2,0:T(8,128)(2,1)S(1)}, bf16[1,2048,704]{1,2,0:T(8,128)(2,1)}, u32[]{:S(2)}) copy-start(bf16[1,2048,704]{1,2,0:T(8,128)(2,1)} %param.26) | copy-start | bytes 8650756
  272.7 7.6 %copy-start.9 = (f32[128,6]{0,1:T(8,128)S(1)}, f32[128,6]{0,1:T(8,128)}, u32[]{:S(2)}) copy-start(f32[128,6]{0,1:T(8,128)} %param.29) | copy-start | bytes 9220
  272.7 67.5 %all-to-all-start.1 = ((bf16[16,36,2048]{2,1,0:T(8,128)(2,1)}), bf16[16,36,2048]{2,1,0:T(8,128)(2,1)}, u32[]{:S(2)}, u32[]{:S(2)}) async-start(bf16[16,36,2048]{2,1,0:T(8,128)(2,1)} %reshape.571), calls=%async_computation.3 | async-start | bytes 5242880 | tf_op jit(solution)/shard_map/all_to_all | solution.py:168
  355.2 3.8 %copy-start.5 = (bf16[64,2048]{1,0:T(8,128)(2,1)S(1)}, bf16[64,2048]{1,0:T(8,128)(2,1)}, u32[]{:S(2)}) copy-start(bf16[64,2048]{1,0:T(8,128)(2,1)} %reduce-scatter.3.cloned.1.call-done) | copy-start | bytes 786436
Sparse Core Ops, SparseCore 0:
  13.5 62.8 all-gather.2
  108.7 15.7 reduce-scatter.2
  208.6 14.6 all-gather.4
  254.8 13.7 reduce-scatter.4
where the time goes:
time: 372 us; the launch traced here: 367 us
  waiting for transfers between devices  102 us (27%)
  blocking collectives  99.7 us (27%)
  local copies, waits for them, and re-layouts  59.6 us (16%)
  matrix products  48 us (13%)
  other arithmetic  35.6 us (10%)
  between operations  14 us (4%)
  starting transfers between devices  8.14 us (2%)
    all_to_all x1, blocking collectives, body(): lax.all_to_all(packed, 'seq', split_axis=0, concat_axis=0, tiled=True)  65.4 us
    all_to_all x1, waiting for transfers between devices, body(): lax.all_to_all(expert_out, 'seq', split_axis=0, concat_axis=0, tiled=True)  59.8 us
    all_gather x1, blocking collectives, body(): piece_rope = lax.all_gather(key_rope, 'seq', axis=0, tiled=True)  31.8 us
    add x1, other arithmetic, positions(): return block_num * half_width + within % half_width  15.7 us
    all_gather x1, waiting for transfers between devices, body(): piece_data = lax.all_gather(arrived, 'tp', axis=0, tiled=True)  14.5 us
    reduce_scatter x1, waiting for transfers between devices, body(): lax.psum_scatter(jnp.dot(hidden, down_local, preferred_element_type=jnp.f...  13.9 us
    reduce_scatter x1, waiting for transfers between devices, body(): lax.psum_scatter(partial_out.astype(jnp.bfloat16), 'tp', scatter_dimensio...  13.6 us
    scatter x1, local copies, waits for them, and re-layouts, body(): buffer = jnp.zeros((seq_count * capacity, model_dim), jnp.bfloat16).at[ta...  9.53 us
  transfers between devices with their start and end apart: 5, of which 4 were waited for; matrix products, arithmetic and copies ran while one was open for 10% of the time, Pallas kernels for 0%

commit v1 on v0

--- a/solution.py
+++ b/solution.py
@@ -3,6 +3,8 @@
 import jax
 import jax.numpy as jnp
 from jax import lax
+from jax.experimental import pallas as pl
+from jax.experimental.pallas import tpu as pltpu
 from jax.sharding import PartitionSpec as P
 
 EPSILON = 1e-06
@@ -43,7 +45,7 @@
     return block_num * half_width + within % half_width
 
 
-def body(
+def plain_body(
     tokens,
     block_ids,
     attn_gain,
@@ -175,9 +177,575 @@
     return (mixed_rows.astype(jnp.float32) + combined).astype(jnp.bfloat16)
 
 
+PLANE = 4
+GROUPS = ((0,), (1, 3), (2,))
+F32 = jnp.float32
+BF16 = jnp.bfloat16
+
+
+def params(megabytes):
+    return pltpu.CompilerParams(vmem_limit_bytes=megabytes * 1024 * 1024)
+
+
+def cost(flops, bytes_accessed, transcendentals=0):
+    return pl.CostEstimate(
+        flops=int(flops), bytes_accessed=int(bytes_accessed), transcendentals=int(transcendentals)
+    )
+
+
+def vmem():
+    return pl.BlockSpec(memory_space=pltpu.VMEM)
+
+
+def smem():
+    return pl.BlockSpec(memory_space=pltpu.SMEM)
+
+
+def anywhere():
+    return pl.BlockSpec(memory_space=pl.ANY)
+
+
+def shape(rows, columns, dtype):
+    return jax.ShapeDtypeStruct((rows, columns), dtype)
+
+
+def tiles(extent, step):
+    return [(first, min(first + step, extent)) for first in range(0, extent, step)]
+
+
+def whole_tiles(rows):
+    return -(-rows // 16) * 16
+
+
+def swap_halves(values):
+    half = values.shape[-1] // 2
+    return jnp.concatenate([values[:, half:], values[:, :half]], axis=1)
+
+
+def dot_nt(left, right):
+    return lax.dot_general(left, right, (((1,), (1,)), ((), ())), preferred_element_type=F32)
+
+
+def dot(left, right):
+    return jnp.dot(left, right, preferred_element_type=F32)
+
+
+def latent_kernel(
+    block_ids, tokens, gain, weight, kv_gain, routes, gates, out, cosine, sine
+):
+    rows = tokens.shape[0]
+    latent_dim = kv_gain.shape[1]
+    rope_dim = cosine.shape[1]
+    core = lax.axis_index("tp")
+    place = lax.axis_index("seq")
+    row = lax.broadcasted_iota(jnp.int32, (2 * rows, 1), 0)
+    block = jnp.where(row < rows, block_ids[0, place], block_ids[1, place])
+    pos = (block * rows + row % rows).astype(F32)
+    lane = lax.broadcasted_iota(jnp.int32, (1, rope_dim // 2), 1).astype(F32)
+    angles = pos * jnp.exp(lane * (-2.0 * math.log(10000.0) / rope_dim))
+    cos_part, sin_part = jnp.cos(angles), jnp.sin(angles)
+    cosine[...] = jnp.concatenate([cos_part, cos_part], axis=1)
+    sine[...] = jnp.concatenate([-sin_part, sin_part], axis=1)
+
+    normed = normalize(tokens[...], gain[...]).astype(BF16)
+    projected = dot_nt(normed, weight[...])
+    latent = normalize(projected[:, :latent_dim], kv_gain[...])
+    rope = projected[:, latent_dim:]
+    own = pl.ds(pl.multiple_of(core * rows, rows), rows)
+    rope = rope * cosine[own, :] + swap_halves(rope) * sine[own, :]
+
+    gate = gates[...]
+    first = gate.astype(BF16)
+    rest = gate - first.astype(F32)
+    second = rest.astype(BF16)
+    third = (rest - second.astype(F32)).astype(BF16)
+    info = jnp.concatenate(
+        [routes[...].astype(F32)] + [part.astype(F32) for part in (first, second, third)], axis=0
+    ).astype(BF16)
+    at_row = lax.broadcasted_iota(jnp.int32, (rows, 2 * rows), 0)
+    at_col = lax.broadcasted_iota(jnp.int32, (rows, 2 * rows), 1)
+    info = dot_nt((at_col == at_row + core * rows).astype(BF16), info)
+    spare = out.shape[1] - latent_dim - rope_dim - info.shape[1]
+    out[:, :latent_dim] = latent.astype(BF16)
+    out[:, latent_dim:] = jnp.concatenate(
+        [rope, info, jnp.zeros((rows, spare), F32)], axis=1
+    ).astype(BF16)
+
+
+def query_kernel(own, other, gain, cosine, sine, q_weight, uk_weight, low, high, normed):
+    rows = own.shape[0]
+    heads, latent_dim, nope = uk_weight.shape
+    rope_dim = cosine.shape[1]
+
+    @pl.when(pl.program_id(0) == 0)
+    def _():
+        core = lax.axis_index("tp")
+        normed[pl.ds(pl.multiple_of(core * rows, rows), rows), :] = normalize(
+            own[...], gain[...]
+        ).astype(BF16)
+        normed[pl.ds(pl.multiple_of((1 - core) * rows, rows), rows), :] = normalize(
+            other[...], gain[...]
+        ).astype(BF16)
+
+    queries = dot(normed[...], q_weight[...]).astype(BF16)
+    for head in range(heads):
+        first = head * (nope + rope_dim)
+        latent = dot_nt(queries[:, first : first + nope], uk_weight[head]).astype(BF16)
+        rope = queries[:, first + nope : first + nope + rope_dim].astype(F32)
+        rope = rope * cosine[...] + swap_halves(rope) * sine[...]
+        rope = jnp.concatenate([rope, jnp.zeros_like(rope)], axis=1).astype(BF16)
+        here = slice(head * rows, (head + 1) * rows)
+        low[here, :latent_dim] = latent[:rows]
+        low[here, latent_dim:] = rope[:rows]
+        high[here, :latent_dim] = latent[rows:]
+        high[here, latent_dim:] = rope[rows:]
+
+
+def attention_kernel(scale, order, pieces, *refs):
+    block_ids, low, high = refs[:3]
+    piece_refs = refs[3 : 3 + 2 * pieces]
+    uv_hbm, o_hbm, keep, send = refs[3 + 2 * pieces : 7 + 2 * pieces]
+    keys, uv, o, out_low, out_high, head_out, total, key_sems, w_sems = refs[7 + 2 * pieces :]
+    me = lax.axis_index("tp")
+    place = lax.axis_index("seq")
+    copies = []
+    first = 0
+    for i, piece in enumerate(piece_refs):
+        side = me if i < pieces else 1 - me
+        first = 0 if i == pieces else first
+        size = piece.shape[0]
+        copies.append(
+            pltpu.make_async_copy(piece, keys.at[side, pl.ds(first, size)], key_sems.at[i])
+        )
+        first += size
+    uv_copy = pltpu.make_async_copy(uv_hbm, uv, w_sems.at[0])
+    o_copy = pltpu.make_async_copy(o_hbm, o, w_sems.at[1])
+    for copy in copies:
+        copy.start()
+    uv_copy.start()
+    o_copy.start()
+    heads, latent_dim, value_dim = uv.shape
+    query_rows = low.shape[0]
+    rows = query_rows // heads
+    layers = block_ids.shape[1] // PLANE
+    key_lane = lax.broadcasted_iota(jnp.int32, (1, len(order) * rows), 1)
+    key_block = [jnp.zeros_like(key_lane), jnp.zeros_like(key_lane)]
+    layer, inner = place // PLANE, place % PLANE
+    for i, (j, k) in enumerate(order):
+        source = lax.rem(layer + layers - k, layers) * PLANE + (inner ^ j)
+        for side in range(2):
+            key_block[side] = jnp.where(
+                key_lane // rows == i, block_ids[side, source], key_block[side]
+            )
+    for copy in copies:
+        copy.wait()
+    tile = min(256, query_rows)
+    within = lax.broadcasted_iota(jnp.int32, (tile, 1), 0) % rows
+    for first in range(0, query_rows, tile):
+        here = slice(first, first + tile)
+        for queries, side, out in ((low, 0, out_low), (high, 1, out_high)):
+            q = queries[here, :]
+            key_pos = key_block[side] * rows + key_lane % rows
+            allowed = key_pos <= block_ids[side, place] * rows + within
+            masked = jnp.where(allowed, dot_nt(q, keys[side]), -1e30)
+            top = jnp.max(masked, axis=1, keepdims=True)
+            if side == 1:
+                plain = dot_nt(q, keys[0])
+                top = jnp.maximum(top, jnp.max(plain, axis=1, keepdims=True))
+            terms = jnp.exp((masked - top) * scale)
+            row_sum = jnp.sum(terms, axis=1, keepdims=True)
+            mixed = dot(terms.astype(BF16), keys[side, :, :latent_dim])
+            if side == 1:
+                terms = jnp.exp((plain - top) * scale)
+                row_sum = row_sum + jnp.sum(terms, axis=1, keepdims=True)
+                mixed = mixed + dot(terms.astype(BF16), keys[0, :, :latent_dim])
+            out[here, :] = (mixed / row_sum).astype(BF16)
+    uv_copy.wait()
+    for head in range(heads):
+        here = slice(head * rows, (head + 1) * rows)
+        both = jnp.concatenate([out_low[here, :], out_high[here, :]], axis=0)
+        head_out[:, head * value_dim : (head + 1) * value_dim] = dot(both, uv[head]).astype(BF16)
+    o_copy.wait()
+    for first, last in tiles(o.shape[1], 512):
+        total[:, first:last] = dot(head_out[...], o[:, first:last])
+    keep[...] = total[pl.ds(pl.multiple_of(me * rows, rows), rows), :]
+    send[...] = total[pl.ds(pl.multiple_of((1 - me) * rows, rows), rows), :].astype(BF16)
+
+
+def mixed_kernel(tokens, keep, received, gain, mixed, normed):
+    attn = keep[...] + received[...].astype(F32)
+    rounded = (tokens[...].astype(F32) + attn).astype(BF16)
+    mixed[...] = rounded
+    normed[...] = normalize(rounded, gain[...]).astype(BF16)
+
+
+def table_kernel(capacity, rows, top, info_at, *refs):
+    blocks = refs[0]
+    slot_rows, slot_cols, gate_cols = (refs[1 + i :: 3] for i in range(3))
+    dests = slot_rows[0].shape[0]
+    place = lax.axis_index("seq")
+    at_row = lax.broadcasted_iota(jnp.int32, (rows, rows), 0)
+    at_col = lax.broadcasted_iota(jnp.int32, (rows, rows), 1)
+    before = (at_col < at_row).astype(BF16)
+    same = (at_col == at_row).astype(BF16)
+    lane = lax.broadcasted_iota(jnp.int32, (rows, dests), 1)
+    for g, group in enumerate(GROUPS):
+        for i, k in enumerate(group):
+            block = blocks[k * rows : (k + 1) * rows, info_at:].astype(F32)
+            routes = block[:, :top]
+            gates = block[:, top : 2 * top] + block[:, 2 * top : 3 * top]
+            gates = gates + block[:, 3 * top : 4 * top]
+            named = jnp.zeros((rows, dests), F32)
+            gate = jnp.zeros((rows, dests), F32)
+            for j in range(dests):
+                expert = place // PLANE * PLANE + (place % PLANE ^ j)
+                hit = (routes == expert.astype(F32)).astype(F32)
+                named = jnp.where(lane == j, jnp.sum(hit, axis=1, keepdims=True), named)
+                gate = jnp.where(lane == j, jnp.sum(hit * gates, axis=1, keepdims=True), gate)
+            rank = dot(before, named.astype(BF16))
+            slot = jnp.where(named > 0.5, rank + float(i * capacity), -1.0)
+            here = slice(i * rows, (i + 1) * rows)
+            slot_cols[g][here, :] = slot
+            gate_cols[g][here, :] = gate
+            slot_rows[g][:, here] = lax.dot_general(
+                slot.astype(BF16), same, (((0,), (0,)), ((), ())), preferred_element_type=F32
+            )
+
+
+def pack_kernel(*refs):
+    dests = refs[0].shape[0]
+    slot_rows, blocks, outs = refs[0], refs[1:-dests], refs[-dests:]
+    packed = outs[0].shape[0]
+    stride = whole_tiles(packed)
+    values = [block[...] for block in blocks]
+    if len(values) * values[0].shape[0] > slot_rows.shape[1]:
+        from_below = lax.axis_index("seq") // PLANE >= 2
+        values = [jnp.where(from_below, values[0], values[1])]
+    values = jnp.concatenate(values, axis=0)
+    place = lax.broadcasted_iota(jnp.int32, (stride, values.shape[0]), 0).astype(F32)
+    picks = [(place == slot_rows[j : j + 1, :]).astype(BF16) for j in range(dests)]
+    picked = dot(jnp.concatenate(picks, axis=0), values).astype(BF16)
+    for j, out in enumerate(outs):
+        out[...] = picked[j * stride : j * stride + packed, :]
+
+
+def expert_kernel(*refs):
+    rows_got, weights, outs = refs[:PLANE], refs[PLANE : PLANE + 6], refs[PLANE + 6 : 2 * PLANE + 6]
+    staged, gate_w, up_w, down_w, sems = refs[2 * PLANE + 6 :]
+    copies = []
+    for half in range(2):
+        for kind, held in enumerate((gate_w, up_w, down_w)):
+            copies.append(
+                pltpu.make_async_copy(
+                    weights[3 * half + kind].at[0], held.at[half], sems.at[half, kind]
+                )
+            )
+    for i in (0, 1, 3, 4, 2, 5):
+        copies[i].start()
+    packed = rows_got[0].shape[0]
+    for j, piece in enumerate(rows_got):
+        staged[j * packed : (j + 1) * packed, :] = piece[...].astype(F32)
+    rows_in = staged[...].astype(BF16)
+    hidden = []
+    for half in range(2):
+        copies[3 * half].wait()
+        gate = dot_nt(rows_in, gate_w[half])
+        copies[3 * half + 1].wait()
+        up = dot_nt(rows_in, up_w[half])
+        hidden.append((gate / (1.0 + jnp.exp(-gate)) * up).astype(BF16))
+    copies[2].wait()
+    value = dot(hidden[0], down_w[0])
+    copies[5].wait()
+    staged[...] = value + dot(hidden[1], down_w[1])
+    for j, out in enumerate(outs):
+        out[...] = staged[j * packed : (j + 1) * packed, :].astype(BF16)
+
+
+def unpack_kernel(slot_cols, gate_cols, *refs):
+    dests = slot_cols.shape[1]
+    values, outs = refs[:dests], refs[dests:]
+    packed = values[0].shape[0]
+    rows = outs[0].shape[0]
+    place = lax.broadcasted_iota(jnp.int32, (slot_cols.shape[0], packed), 1).astype(F32)
+    total = None
+    for j, value in enumerate(values):
+        pick = (place == slot_cols[:, j : j + 1]).astype(BF16)
+        term = dot(pick, value[...]) * gate_cols[:, j : j + 1]
+        total = term if total is None else total + term
+    for i, out in enumerate(outs):
+        out[...] = total[i * rows : (i + 1) * rows].astype(out.dtype)
+
+
+def final_kernel(mixed, own, *refs):
+    total = own[...]
+    for ref in refs[:-1]:
+        total = total + ref[...].astype(F32)
+    refs[-1][...] = (mixed[...].astype(F32) + total).astype(BF16)
+
+
+def fast_body(
+    tokens,
+    block_ids,
+    attn_gain,
+    q_weight,
+    kv_weight,
+    kv_gain,
+    uk_weight,
+    uv_weight,
+    o_weight,
+    ffn_gain,
+    w_gate,
+    w_up,
+    w_down,
+    routes,
+    gate_weights,
+):
+    seq_count = lax.axis_size("seq")
+    layers = seq_count // PLANE
+    rows, model_dim = tokens.shape
+    heads, latent_dim, nope_dim = uk_weight.shape
+    rope_dim = kv_weight.shape[1] - latent_dim
+    value_dim = uv_weight.shape[2]
+    top_count = routes.shape[1]
+    units = w_gate.shape[2]
+    capacity = min(rows, max(2, 3 * rows * top_count // (2 * seq_count)))
+    key_width = latent_dim + 2 * rope_dim
+    scale = (nope_dim + rope_dim) ** (-0.5)
+    barrier = lax.optimization_barrier
+
+    def along(values, step):
+        pairs = [
+            (s, ((s // PLANE + step) % layers) * PLANE + s % PLANE) for s in range(seq_count)
+        ]
+        return lax.ppermute(values, "seq", pairs)
+
+    def forward(values, step):
+        pairs = [
+            (s, s + step * PLANE)
+            for s in range(seq_count)
+            if 0 < s // PLANE < layers - 1
+        ]
+        return lax.ppermute(values, "seq", pairs)
+
+    def across(values, j):
+        return lax.ppermute(values, "seq", [(s, s ^ j) for s in range(seq_count)])
+
+    def swap(values):
+        return lax.ppermute(values, "tp", [(0, 1), (1, 0)])
+
+    def call(kernel, name, megabytes, flops, bytes_accessed, **options):
+        return pl.pallas_call(
+            kernel,
+            compiler_params=params(megabytes),
+            cost_estimate=cost(flops, bytes_accessed),
+            name=name,
+            **options,
+        )
+
+    attn_gain = attn_gain.reshape(1, model_dim)
+    kv_gain = kv_gain.reshape(1, latent_dim)
+    ffn_gain = ffn_gain.reshape(1, model_dim)
+
+    other_tokens = swap(tokens)
+    gate_t, up_t = jnp.swapaxes(w_gate, 1, 2), jnp.swapaxes(w_up, 1, 2)
+    gate_other, up_other = swap(gate_t), swap(up_t)
+
+    latents, cosine, sine = call(
+        latent_kernel,
+        "own_latents",
+        56,
+        2 * rows * model_dim * key_width,
+        kv_weight.size * 2,
+        out_shape=(
+            shape(rows, key_width, BF16),
+            shape(2 * rows, rope_dim, F32),
+            shape(2 * rows, rope_dim, F32),
+        ),
+        in_specs=[smem()] + [vmem()] * 6,
+        out_specs=(vmem(),) * 3,
+    )(block_ids.T, tokens, attn_gain, kv_weight.T, kv_gain, routes.T, gate_weights.T)
+
+    column_keys = jnp.concatenate(
+        [latents] + [along(latents, k) for k in range(1, layers)], axis=0
+    )
+    far = [across(column_keys, j) for j in range(1, PLANE)]
+    other_tokens, cosine, sine, behind = barrier((other_tokens, cosine, sine, column_keys))
+
+    pair = 2
+    low, high = call(
+        query_kernel,
+        "queries",
+        20,
+        4 * rows * (q_weight.size + uk_weight.size),
+        2 * (q_weight.size + uk_weight.size),
+        grid=(heads // pair,),
+        out_shape=(shape(heads * rows, key_width, BF16),) * 2,
+        in_specs=[vmem()] * 5
+        + [
+            pl.BlockSpec((model_dim, pair * (nope_dim + rope_dim)), lambda i: (0, i)),
+            pl.BlockSpec((pair, latent_dim, nope_dim), lambda i: (i, 0, 0)),
+        ],
+        out_specs=(pl.BlockSpec((pair * rows, key_width), lambda i: (i, 0)),) * 2,
+        scratch_shapes=[pltpu.VMEM((2 * rows, model_dim), BF16)],
+    )(tokens, other_tokens, attn_gain, cosine, sine, q_weight, uk_weight)
+
+    column = layers * rows
+    slots = call(
+        lambda *refs: table_kernel(capacity, rows, top_count, latent_dim + rope_dim, *refs),
+        "row_tables",
+        8,
+        column * rows * 8,
+        column * 128 * 12,
+        out_shape=tuple(
+            part
+            for group in GROUPS
+            for part in (
+                shape(PLANE, len(group) * rows, F32),
+                shape(len(group) * rows, PLANE, F32),
+                shape(len(group) * rows, PLANE, F32),
+            )
+        ),
+        in_specs=[vmem()],
+        out_specs=(vmem(),) * (3 * len(GROUPS)),
+    )(behind)
+    far, low, high, slots, gate_other = barrier((far, low, high, slots, gate_other))
+    own_keys = [column_keys] + far
+    other_keys = [swap(piece) for piece in own_keys]
+    order = [(j, k) for j in range(PLANE) for k in range(layers)]
+
+    *other_keys, ready = barrier((*other_keys, w_down))
+    down_other = swap(ready)
+
+    keep, send = call(
+        lambda *refs: attention_kernel(scale, order, len(own_keys), *refs),
+        "attention",
+        28,
+        3 * 2 * heads * rows * seq_count * rows * (key_width + latent_dim),
+        2 * (o_weight.size + uv_weight.size),
+        out_shape=(shape(rows, model_dim, F32), shape(rows, model_dim, BF16)),
+        in_specs=[smem(), vmem(), vmem()] + [anywhere()] * (2 * len(own_keys) + 2),
+        out_specs=(vmem(), vmem()),
+        scratch_shapes=[
+            pltpu.VMEM((2, seq_count * rows, key_width), BF16),
+            pltpu.VMEM(uv_weight.shape, BF16),
+            pltpu.VMEM(o_weight.shape, BF16),
+            pltpu.VMEM((heads * rows, latent_dim), BF16),
+            pltpu.VMEM((heads * rows, latent_dim), BF16),
+            pltpu.VMEM((2 * rows, heads * value_dim), BF16),
+            pltpu.VMEM((2 * rows, model_dim), F32),
+            pltpu.SemaphoreType.DMA((2 * len(own_keys),)),
+            pltpu.SemaphoreType.DMA((2,)),
+        ],
+    )(block_ids.T, low, high, *own_keys, *other_keys, uv_weight, o_weight)
+    received, gate_other, up_other, down_other = barrier(
+        (swap(send), gate_other, up_other, down_other)
+    )
+
+    mixed, normed = call(
+        mixed_kernel,
+        "mixed_rows",
+        8,
+        rows * model_dim * 8,
+        rows * model_dim * 12,
+        out_shape=(shape(rows, model_dim, BF16),) * 2,
+        in_specs=[vmem()] * 4,
+        out_specs=(vmem(),) * 2,
+    )(tokens, keep, received, ffn_gain)
+
+    def expert(got):
+        packed = got[0].shape[0]
+        return call(
+            expert_kernel,
+            "expert",
+            40,
+            0,
+            0,
+            out_shape=(shape(packed, model_dim, BF16),) * PLANE,
+            in_specs=[vmem()] * PLANE + [anywhere()] * 6,
+            out_specs=(vmem(),) * PLANE,
+            scratch_shapes=[
+                pltpu.VMEM((PLANE * packed, model_dim), F32),
+                pltpu.VMEM((2,) + gate_t.shape[1:], BF16),
+                pltpu.VMEM((2,) + gate_t.shape[1:], BF16),
+                pltpu.VMEM((2,) + w_down.shape[1:], BF16),
+                pltpu.SemaphoreType.DMA((2, 3)),
+            ],
+        )(*got, gate_t, up_t, w_down, gate_other, up_other, down_other)
+
+    beside = {k: along(normed, k) for k in (1, layers - 1)}
+    arrivals = [[normed], list(beside.values()), []]
+    pieces = []
+    for g, group in enumerate(GROUPS):
+        packed = len(group) * capacity
+        if g == 2:
+            above, below, *_ = barrier((beside[1], beside[layers - 1], *pieces[0]))
+            arrivals[2] = [forward(above, 1), forward(below, -1)]
+            expert_outs = [expert(pieces[0])]
+            arrivals[2], *_ = barrier((arrivals[2], *expert_outs[0]))
+        outs = call(
+            pack_kernel,
+            "pack_rows",
+            12,
+            0,
+            0,
+            out_shape=(shape(packed, model_dim, BF16),) * PLANE,
+            in_specs=[vmem()] * (1 + len(arrivals[g])),
+            out_specs=(vmem(),) * PLANE,
+        )(slots[3 * g], *arrivals[g])
+        if g == 1:
+            own, *outs = barrier((pieces[0][0], *outs))
+            pieces[0][0] = own
+        pieces.append([outs[0]] + [across(outs[j], j) for j in range(1, PLANE)])
+
+    for got in pieces[1:]:
+        got, *_ = barrier((got, *expert_outs[-1]))
+        expert_outs.append(expert(got))
+
+    sums, done = [None] * layers, []
+    for g in (1, 2, 0):
+        group, outs = GROUPS[g], expert_outs[g]
+        if g == 1:
+            outs, *_ = barrier((list(outs), *pieces[2]))
+        if g == 0:
+            outs, *_ = barrier((list(outs), *done, sums[1], sums[layers - 1]))
+        returned = [across(outs[j], j) for j in range(1, PLANE)]
+        if g == 1:
+            returned, *_ = barrier((returned, *expert_outs[2]))
+        results = call(
+            unpack_kernel,
+            "unpack_rows",
+            12,
+            0,
+            0,
+            out_shape=tuple(shape(rows, model_dim, BF16 if k else F32) for k in group),
+            in_specs=[vmem()] * (2 + PLANE),
+            out_specs=(vmem(),) * len(group),
+        )(
+            slots[3 * g + 1],
+            slots[3 * g + 2],
+            outs[0],
+            *returned,
+        )
+        done += results
+        for k, result in zip(group, results):
+            sums[k] = along(result, -k) if k else result
+
+    return call(
+        final_kernel,
+        "layer_out",
+        8,
+        rows * model_dim * 8,
+        rows * model_dim * 14,
+        out_shape=shape(rows, model_dim, BF16),
+        in_specs=[vmem()] * (1 + layers),
+        out_specs=vmem(),
+    )(mixed, *sums)
+
+
 def solution(mesh):
+    fits = mesh.shape["tp"] == 2 and mesh.shape["seq"] == 4 * PLANE
     return jax.shard_map(
-        body,
+        fast_body if fits else plain_body,
         mesh=mesh,
         in_specs=(
             P(("seq", "tp"), None),

time: 372 us -> 140 us (0.38)
  the two profiles are of different devices: /device:TPU:14 before, /device:TPU:0 now
where the time goes in v1:
time: 140 us; the launch traced here: 139 us
  Pallas kernels  46.4 us (33%)
  starting transfers between devices  45.1 us (32%)
  waiting for transfers between devices  38.4 us (27%)
  local copies, waits for them, and re-layouts  9.26 us (7%)
    ppermute x21, starting transfers between devices, across(): return lax.ppermute(values, 'seq', [(s, s ^ j) for s in range(seq_count)])  24.8 us
    pallas_call x3, Pallas kernels, expert(): call(expert_kernel, 'expert', 40, 0, 0, out_shape=(shape(packed, model_di...  23.4 us
    ppermute x21, waiting for transfers between devices, across(): return lax.ppermute(values, 'seq', [(s, s ^ j) for s in range(seq_count)])  20.2 us
    ppermute x8, starting transfers between devices, along(): return lax.ppermute(values, 'seq', pairs)  16 us
    ppermute x8, waiting for transfers between devices, along(): return lax.ppermute(values, 'seq', pairs)  15.5 us
    unnamed x33, local copies, waits for them, and re-layouts  9.25 us
    pallas_call x1, Pallas kernels, fast_body(): call(lambda *refs: attention_kernel(scale, order, len(own_keys), *refs),...  8.62 us
    pallas_call x1, Pallas kernels, fast_body(): call(query_kernel, 'queries', 20, 4 * rows * (q_weight.size + uk_weight.s...  3.8 us
  transfers between devices with their start and end apart: 40, of which 17 were waited for; matrix products, arithmetic and copies ran while one was open for 1% of the time, Pallas kernels for 32%

profile of v1, /device:TPU:0, one launch (start us, length us, event | category | flops | bytes accessed | tf_op | source)
XLA Modules:
  0.0 139.4 jit_solution(14786999144030292935)
XLA Ops:
  0.0 0.5 collective-permute-start.7
  0.5 3.6 %own_latents.1 = (bf16[64,640]{1,0:T(8,128)(2,1)}, f32[128,64]{1,0:T(8,128)}, f32[128,64]{1,0:T(8,128)}) custom-call(s32[2,16]{1,0:T(2,128)} %bitcast.20, bf16[64,2048]{1,0:T(8,128)(2,1)} %tokens.3, f32[1,2048]{1,0:T(1,128)} %bitcast.17, bf16[576,2048]{1,0:T(8,128)(2,1)} %bitcast.22, f32[1,512]{1,0:T(1,128)} %bitcast.25, s32[6,128]{1,0:T(8,128)} %bitcast.23, ...), custom_call_target="tpu_custom_call" | custom-call | flops 167772160 | bytes 2359296 | tf_op jit(solution)/shard_map/own_latents/pallas_call | solution.py:553
  4.1 4.7 %collective-permute-start.2 = (bf16[64,640]{1,0:T(8,128)(2,1)}, bf16[64,640]{1,0:T(8,128)(2,1)S(1)}, u32[]{:S(2)}, u32[]{:S(2)}) collective-permute-start(bf16[64,640]{1,0:T(8,128)(2,1)} %get-tuple-element.105), channel_id=1, source_target_pairs={{0,24},{2,26},{4,28},{6,30},{8,0},{10,2},{12,4},{14,6},{16,8},{18,... | collective-permute-start | bytes 245768 | tf_op jit(solution)/shard_map/ppermute | solution.py:520
  8.8 1.0 collective-permute-start
  9.8 0.9 constant_dynamic-update-slice_fusion.3
  10.7 5.1 %collective-permute-done = bf16[64,640]{1,0:T(8,128)(2,1)S(1)} collective-permute-done((bf16[64,640]{1,0:T(8,128)(2,1)}, bf16[64,640]{1,0:T(8,128)(2,1)S(1)}, u32[]{:S(2)}, u32[]{:S(2)}) %collective-permute-start) | collective-permute-done | bytes 81952 | tf_op jit(solution)/shard_map/ppermute | solution.py:520
  15.8 1.6 %collective-permute-done.1 = bf16[64,640]{1,0:T(8,128)(2,1)S(1)} collective-permute-done((bf16[64,640]{1,0:T(8,128)(2,1)}, bf16[64,640]{1,0:T(8,128)(2,1)S(1)}, u32[]{:S(2)}, u32[]{:S(2)}) %collective-permute-start.1) | collective-permute-done | bytes 81952 | tf_op jit(solution)/shard_map/ppermute | solution.py:520
  17.5 2.5 %collective-permute-start.5 = (bf16[256,640]{1,0:T(8,128)(2,1)S(1)}, bf16[256,640]{1,0:T(8,128)(2,1)S(1)}, u32[]{:S(2)}, u32[]{:S(2)}) collective-permute-start(bf16[256,640]{1,0:T(8,128)(2,1)S(1)} %constant_dynamic-update-slice_fusion.refs_0_.refs_3_), channel_id=1, source_target_pairs={{0,6},{2,4},{4,2},{6,0},{8,14},{10,12},{12,10},{14,8},{16,22},{18,... | collective-permute-start | bytes 983048 | tf_op jit(solution)/shard_map/ppermute | solution.py:531
  20.0 0.5 collective-permute-start.4
  20.5 0.5 collective-permute-start.3
  21.1 3.0 %row_tables.1 = (f32[4,64]{1,0:T(4,128)S(1)}, f32[64,4]{1,0:T(8,128)S(1)}, f32[64,4]{1,0:T(8,128)S(1)}, f32[4,128]{1,0:T(4,128)S(1)}, f32[128,4]{1,0:T(8,128)S(1...) custom-call(bf16[256,640]{1,0:T(8,128)(2,1)S(1)} %constant_dynamic-update-slice_fusio, ...), custom_call_target="tpu_custom_call" | custom-call | flops 131072 | bytes 393216 | tf_op jit(solution)/shard_map/row_tables/pallas_call | solution.py:593
  24.1 2.8 %copy-done.3 = bf16[2048,1536]{1,0:T(8,128)(2,1)S(1)} copy-done((bf16[2048,1536]{1,0:T(8,128)(2,1)S(1)}, bf16[2048,1536]{1,0:T(8,128)(2,1)}, u32[]{:S(2)}) %copy-start.3) | copy-done | bytes 6291480
  26.9 0.8 copy-done.6
  27.7 0.8 copy-done.7
  28.6 3.8 %queries.1 = (bf16[512,640]{1,0:T(8,128)(2,1)S(1)}, bf16[512,640]{1,0:T(8,128)(2,1)S(1)}) custom-call(bf16[64,2048]{1,0:T(8,128)(2,1)S(1)} %copy-done.4, bf16[64,2048]{1,0:T(8,128)(2,1)S(1)} %collective-permute-done.6.other, f32[1,2048]{1,0:T(1,128)S(1)} %bitcast.18, f32[128,64]{1,0:T(8,128)S(1)} %copy-done.6, f32[128,64]{1,0:T(8,128)S(1)} %copy-done.7, ...), custom_call_target="tpu_custom_call" | custom-call | flops 939524096 | bytes 7340032 | tf_op jit(solution)/shard_map/queries/pallas_call | solution.py:575
  32.4 2.7 %collective-permute-done.4.refs_5_ = bf16[256,640]{1,0:T(8,128)(2,1)S(1)} collective-permute-done((bf16[256,640]{1,0:T(8,128)(2,1)S(1)}, bf16[256,640]{1,0:T(8,128)(2,1)S(1)}, u32[]{:S(2)}, u32[]{:S(2)}) %collective-permute-start.4) | collective-permute-done | bytes 327712 | tf_op jit(solution)/shard_map/ppermute | solution.py:531
  35.2 0.5 collective-permute-start.10
  35.7 0.5 collective-permute-start.13
  36.2 0.6 collective-permute-done.9.refs_8_
  37.9 2.2 %copy-done.11 = bf16[1024,2048]{1,0:T(8,128)(2,1)S(1)} copy-done((bf16[1024,2048]{1,0:T(8,128)(2,1)S(1)}, bf16[1024,2048]{1,0:T(8,128)(2,1)}, u32[]{:S(2)}) %copy-start.11) | copy-done | bytes 4194328
  40.1 8.6 %attention.1 = (f32[64,2048]{1,0:T(8,128)S(1)}, bf16[64,2048]{1,0:T(8,128)(2,1)S(1)}) custom-call(s32[2,16]{1,0:T(2,128)S(1)} %bitcast.21, bf16[512,640]{1,0:T(8,128)(2,1)S(1)} %get-tuple-element.123.refs_1_, bf16[512,640]{1,0:T(8,128)(2,1)S(1)} %get-tuple-element.124.refs_2_, bf16[256,640]{1,0:T(8,128)(2,1)S(1)} %constant_dynamic-update-slice_fusion.refs_0_.refs_3_, ...), custom_call_target="tpu_custom_call" | custom-call | flops 3623878656 | bytes 5242880 | tf_op jit(solution)/shard_map/attention/pallas_call | solution.py:619
  49.2 1.2 collective-permute-done.12.received
  50.4 1.6 %copy-done.14 = bf16[1,704,2048]{2,1,0:T(8,128)(2,1)} copy-done((bf16[1,704,2048]{2,1,0:T(8,128)(2,1)}, bf16[1,704,2048]{2,1,0:T(8,128)(2,1)S(1)}, u32[]{:S(2)}) %copy-start.14) | copy-done | bytes 2883608
  52.5 1.8 %collective-permute-start.15 = (bf16[64,2048]{1,0:T(8,128)(2,1)S(1)}, bf16[64,2048]{1,0:T(8,128)(2,1)S(1)}, u32[]{:S(2)}, u32[]{:S(2)}) collective-permute-start(bf16[64,2048]{1,0:T(8,128)(2,1)S(1)} %get-tuple-element.141.refs_1_), channel_id=1, source_target_pairs={{0,8},{2,10},{4,12},{6,14},{8,16},{10,18},{12,20},{14,22},{16,24},... | collective-permute-start | bytes 786440 | tf_op jit(solution)/shard_map/ppermute | solution.py:520
  54.7 1.6 %collective-permute-start.17 = (bf16[36,2048]{1,0:T(8,128)(2,1)S(1)}, bf16[36,2048]{1,0:T(8,128)(2,1)S(1)}, u32[]{:S(2)}, u32[]{:S(2)}) collective-permute-start(bf16[36,2048]{1,0:T(8,128)(2,1)S(1)} %get-tuple-element.149), channel_id=1, source_target_pairs={{0,2},{2,0},{4,6},{6,4},{8,10},{10,8},{12,14},{14,12},{16,18},{18,... | collective-permute-start | bytes 442376 | tf_op jit(solution)/shard_map/ppermute | solution.py:531
  56.2 0.7 collective-permute-start.18
  56.9 1.3 collective-permute-start.19
  58.2 2.7 %collective-permute-done.16.refs_2_ = bf16[64,2048]{1,0:T(8,128)(2,1)S(1)} collective-permute-done((bf16[64,2048]{1,0:T(8,128)(2,1)S(1)}, bf16[64,2048]{1,0:T(8,128)(2,1)S(1)}, u32[]{:S(2)}, u32[]{:S(2)}) %collective-permute-start.16) | collective-permute-done | bytes 262176 | tf_op jit(solution)/shard_map/ppermute | solution.py:520
  60.9 6.2 %collective-permute-done.15.refs_1_ = bf16[64,2048]{1,0:T(8,128)(2,1)S(1)} collective-permute-done((bf16[64,2048]{1,0:T(8,128)(2,1)S(1)}, bf16[64,2048]{1,0:T(8,128)(2,1)S(1)}, u32[]{:S(2)}, u32[]{:S(2)}) %collective-permute-start.15) | collective-permute-done | bytes 262176 | tf_op jit(solution)/shard_map/ppermute | solution.py:520
  67.0 0.5 pack_rows.4
  67.5 1.6 %collective-permute-start.20 = (bf16[72,2048]{1,0:T(8,128)(2,1)S(1)}, bf16[72,2048]{1,0:T(8,128)(2,1)S(1)}, u32[]{:S(2)}, u32[]{:S(2)}) collective-permute-start(bf16[72,2048]{1,0:T(8,128)(2,1)S(1)} %get-tuple-element.162), channel_id=1, source_target_pairs={{0,2},{2,0},{4,6},{6,4},{8,10},{10,8},{12,14},{14,12},{16,18},{18,... | collective-permute-start | bytes 884744 | tf_op jit(solution)/shard_map/ppermute | solution.py:531
  69.1 0.7 collective-permute-start.23
  69.8 1.5 %collective-permute-start.24 = (bf16[64,2048]{1,0:T(8,128)(2,1)S(1)}, bf16[64,2048]{1,0:T(8,128)(2,1)S(1)}, u32[]{:S(2)}, u32[]{:S(2)}) collective-permute-start(bf16[64,2048]{1,0:T(8,128)(2,1)S(1)} %collective-permute-done.16.refs_2_), channel_id=1, source_target_pairs={{8,0},{10,2},{12,4},{14,6},{16,8},{18,10},{20,12},{22,14},{9,1},{1... | collective-permute-start | bytes 786440 | tf_op jit(solution)/shard_map/ppermute | solution.py:528
  71.3 0.8 collective-permute-start.21
  72.1 1.3 collective-permute-start.22
  73.3 7.2 %expert.3 = (bf16[36,2048]{1,0:T(8,128)(2,1)S(1)}, bf16[36,2048]{1,0:T(8,128)(2,1)S(1)}, bf16[36,2048]{1,0:T(8,128)(2,1)S(1)}, bf16[36,2048]{1,0:T(8,128)(2,1)S(1)}) custom-call(bf16[36,2048]{1,0:T(8,128)(2,1)S(1)} %get-tuple-element.148.refs_0_, bf16[36,2048]{1,0:T(8,128)(2,1)S(1)} %collective-permute-done.17.refs_1_, ...), custom_call_target="tpu_custom_call" | custom-call | tf_op jit(solution)/shard_map/expert/pallas_call | solution.py:657
  80.9 1.6 %collective-permute-start.25 = (bf16[36,2048]{1,0:T(8,128)(2,1)S(1)}, bf16[36,2048]{1,0:T(8,128)(2,1)S(1)}, u32[]{:S(2)}, u32[]{:S(2)}) collective-permute-start(bf16[36,2048]{1,0:T(8,128)(2,1)S(1)} %get-tuple-element.179), channel_id=1, source_target_pairs={{0,2},{2,0},{4,6},{6,4},{8,10},{10,8},{12,14},{14,12},{16,18},{18,... | collective-permute-start | bytes 442376 | tf_op jit(solution)/shard_map/ppermute | solution.py:531
  82.5 0.7 collective-permute-start.26
  83.2 1.3 collective-permute-start.27
  84.5 6.6 %collective-permute-done.21.refs_2_ = bf16[72,2048]{1,0:T(8,128)(2,1)S(1)} collective-permute-done((bf16[72,2048]{1,0:T(8,128)(2,1)S(1)}, bf16[72,2048]{1,0:T(8,128)(2,1)S(1)}, u32[]{:S(2)}, u32[]{:S(2)}) %collective-permute-start.21) | collective-permute-done | bytes 294944 | tf_op jit(solution)/shard_map/ppermute | solution.py:531
  91.1 8.8 %expert.4 = (bf16[72,2048]{1,0:T(8,128)(2,1)S(1)}, bf16[72,2048]{1,0:T(8,128)(2,1)S(1)}, bf16[72,2048]{1,0:T(8,128)(2,1)S(1)}, bf16[72,2048]{1,0:T(8,128)(2,1)S(1)}) custom-call(bf16[72,2048]{1,0:T(8,128)(2,1)S(1)} %get-tuple-element.165.refs_0_, bf16[72,2048]{1,0:T(8,128)(2,1)S(1)} %collective-permute-done.20.refs_1_, ...), custom_call_target="tpu_custom_call" | custom-call | tf_op jit(solution)/shard_map/expert/pallas_call | solution.py:657
  99.9 0.6 collective-permute-start.28
  100.5 1.4 %collective-permute-start.29 = (bf16[72,2048]{1,0:T(8,128)(2,1)S(1)}, bf16[72,2048]{1,0:T(8,128)(2,1)S(1)}, u32[]{:S(2)}, u32[]{:S(2)}) collective-permute-start(bf16[72,2048]{1,0:T(8,128)(2,1)S(1)} %get-tuple-element.184), channel_id=1, source_target_pairs={{0,4},{2,6},{4,0},{6,2},{8,12},{10,14},{12,8},{14,10},{16,20},{18,... | collective-permute-start | bytes 884744 | tf_op jit(solution)/shard_map/ppermute | solution.py:531
  102.0 1.5 %collective-permute-start.30 = (bf16[72,2048]{1,0:T(8,128)(2,1)S(1)}, bf16[72,2048]{1,0:T(8,128)(2,1)S(1)}, u32[]{:S(2)}, u32[]{:S(2)}) collective-permute-start(bf16[72,2048]{1,0:T(8,128)(2,1)S(1)} %get-tuple-element.185), channel_id=1, source_target_pairs={{0,6},{2,4},{4,2},{6,0},{8,14},{10,12},{12,10},{14,8},{16,22},{18,... | collective-permute-start | bytes 884744 | tf_op jit(solution)/shard_map/ppermute | solution.py:531
  103.5 7.4 %expert.5 = (bf16[36,2048]{1,0:T(8,128)(2,1)S(1)}, bf16[36,2048]{1,0:T(8,128)(2,1)S(1)}, bf16[36,2048]{1,0:T(8,128)(2,1)S(1)}, bf16[36,2048]{1,0:T(8,128)(2,1)S(1)}) custom-call(bf16[36,2048]{1,0:T(8,128)(2,1)S(1)} %get-tuple-element.186.refs_0_, bf16[36,2048]{1,0:T(8,128)(2,1)S(1)} %collective-permute-done.25.refs_1_, ...), custom_call_target="tpu_custom_call" | custom-call | tf_op jit(solution)/shard_map/expert/pallas_call | solution.py:657
  110.9 0.8 unpack_rows.3
  111.7 1.5 %collective-permute-start.34 = (bf16[64,2048]{1,0:T(8,128)(2,1)S(1)}, bf16[64,2048]{1,0:T(8,128)(2,1)S(1)}, u32[]{:S(2)}, u32[]{:S(2)}) collective-permute-start(bf16[64,2048]{1,0:T(8,128)(2,1)S(1)} %get-tuple-element.197), channel_id=1, source_target_pairs={{0,24},{2,26},{4,28},{6,30},{8,0},{10,2},{12,4},{14,6},{16,8},{18,... | collective-permute-start | bytes 786440 | tf_op jit(solution)/shard_map/ppermute | solution.py:520
  113.2 2.1 %collective-permute-start.35 = (bf16[64,2048]{1,0:T(8,128)(2,1)S(1)}, bf16[64,2048]{1,0:T(8,128)(2,1)S(1)}, u32[]{:S(2)}, u32[]{:S(2)}) collective-permute-start(bf16[64,2048]{1,0:T(8,128)(2,1)S(1)} %get-tuple-element.198), channel_id=1, source_target_pairs={{0,8},{2,10},{4,12},{6,14},{8,16},{10,18},{12,20},{14,22},{16,24},... | collective-permute-start | bytes 786440 | tf_op jit(solution)/shard_map/ppermute | solution.py:520
  115.4 1.0 collective-permute-start.31
  116.4 0.7 collective-permute-start.32
  117.1 1.8 %collective-permute-start.33 = (bf16[36,2048]{1,0:T(8,128)(2,1)S(1)}, bf16[36,2048]{1,0:T(8,128)(2,1)S(1)}, u32[]{:S(2)}, u32[]{:S(2)}) collective-permute-start(bf16[36,2048]{1,0:T(8,128)(2,1)S(1)} %get-tuple-element.193), channel_id=1, source_target_pairs={{0,6},{2,4},{4,2},{6,0},{8,14},{10,12},{12,10},{14,8},{16,22},{18,... | collective-permute-start | bytes 442376 | tf_op jit(solution)/shard_map/ppermute | solution.py:531
  118.8 1.8 %collective-permute-done.31.refs_1_ = bf16[36,2048]{1,0:T(8,128)(2,1)S(1)} collective-permute-done((bf16[36,2048]{1,0:T(8,128)(2,1)S(1)}, bf16[36,2048]{1,0:T(8,128)(2,1)S(1)}, u32[]{:S(2)}, u32[]{:S(2)}) %collective-permute-start.31) | collective-permute-done | bytes 147488 | tf_op jit(solution)/shard_map/ppermute | solution.py:531
  120.7 1.2 collective-permute-done.32.refs_2_
  121.8 3.2 %collective-permute-done.33.refs_3_ = bf16[36,2048]{1,0:T(8,128)(2,1)S(1)} collective-permute-done((bf16[36,2048]{1,0:T(8,128)(2,1)S(1)}, bf16[36,2048]{1,0:T(8,128)(2,1)S(1)}, u32[]{:S(2)}, u32[]{:S(2)}) %collective-permute-start.33) | collective-permute-done | bytes 147488 | tf_op jit(solution)/shard_map/ppermute | solution.py:531
  125.0 0.5 unpack_rows.4
  125.5 4.5 %collective-permute-start.39 = (bf16[64,2048]{1,0:T(8,128)(2,1)S(1)}, bf16[64,2048]{1,0:T(8,128)(2,1)S(1)}, u32[]{:S(2)}, u32[]{:S(2)}) collective-permute-start(bf16[64,2048]{1,0:T(8,128)(2,1)S(1)} %unpack_rows.4), channel_id=1, source_target_pairs={{0,16},{2,18},{4,20},{6,22},{8,24},{10,26},{12,28},{14,30},{16,0},... | collective-permute-start | bytes 786440 | tf_op jit(solution)/shard_map/ppermute | solution.py:520
  130.0 0.8 collective-permute-start.36
  130.8 1.0 collective-permute-start.37
  131.9 1.6 %collective-permute-start.38 = (bf16[36,2048]{1,0:T(8,128)(2,1)S(1)}, bf16[36,2048]{1,0:T(8,128)(2,1)S(1)}, u32[]{:S(2)}, u32[]{:S(2)}) collective-permute-start(bf16[36,2048]{1,0:T(8,128)(2,1)S(1)} %get-tuple-element.204), channel_id=1, source_target_pairs={{0,6},{2,4},{4,2},{6,0},{8,14},{10,12},{12,10},{14,8},{16,22},{18,... | collective-permute-start | bytes 442376 | tf_op jit(solution)/shard_map/ppermute | solution.py:531
  133.5 1.8 %collective-permute-done.36.refs_1_ = bf16[36,2048]{1,0:T(8,128)(2,1)S(1)} collective-permute-done((bf16[36,2048]{1,0:T(8,128)(2,1)S(1)}, bf16[36,2048]{1,0:T(8,128)(2,1)S(1)}, u32[]{:S(2)}, u32[]{:S(2)}) %collective-permute-start.36) | collective-permute-done | bytes 147488 | tf_op jit(solution)/shard_map/ppermute | solution.py:531
  135.3 0.8 collective-permute-done.37.refs_2_
  136.1 1.9 %collective-permute-done.38.refs_3_ = bf16[36,2048]{1,0:T(8,128)(2,1)S(1)} collective-permute-done((bf16[36,2048]{1,0:T(8,128)(2,1)S(1)}, bf16[36,2048]{1,0:T(8,128)(2,1)S(1)}, u32[]{:S(2)}, u32[]{:S(2)}) %collective-permute-start.38) | collective-permute-done | bytes 147488 | tf_op jit(solution)/shard_map/ppermute | solution.py:531
  138.1 0.5 unpack_rows.5.own
  138.6 0.9 layer_out.1
  (65 shorter events, 3.0 us)
Async XLA Ops:
  0.0 24.1 %copy-start.4 = (bf16[64,2048]{1,0:T(8,128)(2,1)S(1)}, bf16[64,2048]{1,0:T(8,128)(2,1)}, u32[]{:S(2)}) copy-start(bf16[64,2048]{1,0:T(8,128)(2,1)} %tokens.3) | copy-start | bytes 786436
  0.0 24.1 %copy-start.8 = (f32[2048]{0:T(1024)S(1)}, f32[2048]{0:T(1024)}, u32[]{:S(2)}) copy-start(f32[2048]{0:T(1024)} %param.17) | copy-start | bytes 24580
  0.0 24.1 %copy-start.5 = (bf16[8,512,128]{2,1,0:T(8,128)(2,1)S(1)}, bf16[8,512,128]{2,1,0:T(8,128)(2,1)}, u32[]{:S(2)}) copy-start(bf16[8,512,128]{2,1,0:T(8,128)(2,1)} %uk_weight.1) | copy-start | bytes 3145732
  0.0 35.2 %collective-permute-start.7 = (bf16[1,704,2048]{2,1,0:T(8,128)(2,1)}, bf16[1,704,2048]{2,1,0:T(8,128)(2,1)S(1)}, u32[]{:S(2)}, u32[]{:S(2)}) collective-permute-start(bf16[1,704,2048]{2,1,0:T(8,128)(2,1)} %bitcast.9), channel_id=1, source_target_pairs={{0,1},{1,0},{2,3},{3,2},{4,5},{5,4},{6,7},{7,6},{8,9},{9,8},{10,11... | collective-permute-start | bytes 8650760 | tf_op jit(solution)/shard_map/ppermute | solution.py:534
  4.1 13.4 %collective-permute-start.2 = (bf16[64,640]{1,0:T(8,128)(2,1)}, bf16[64,640]{1,0:T(8,128)(2,1)S(1)}, u32[]{:S(2)}, u32[]{:S(2)}) collective-permute-start(bf16[64,640]{1,0:T(8,128)(2,1)} %get-tuple-element.105), channel_id=1, source_target_pairs={{0,24},{2,26},{4,28},{6,30},{8,0},{10,2},{12,4},{14,6},{16,8},{18,... | collective-permute-start | bytes 245768 | tf_op jit(solution)/shard_map/ppermute | solution.py:520
  8.8 8.7 %collective-permute-start.1 = (bf16[64,640]{1,0:T(8,128)(2,1)}, bf16[64,640]{1,0:T(8,128)(2,1)S(1)}, u32[]{:S(2)}, u32[]{:S(2)}) collective-permute-start(bf16[64,640]{1,0:T(8,128)(2,1)} %get-tuple-element.105), channel_id=1, source_target_pairs={{0,16},{2,18},{4,20},{6,22},{8,24},{10,26},{12,28},{14,30},{16,0},... | collective-permute-start | bytes 245768 | tf_op jit(solution)/shard_map/ppermute | solution.py:520
  8.8 7.0 %collective-permute-start = (bf16[64,640]{1,0:T(8,128)(2,1)}, bf16[64,640]{1,0:T(8,128)(2,1)S(1)}, u32[]{:S(2)}, u32[]{:S(2)}) collective-permute-start(bf16[64,640]{1,0:T(8,128)(2,1)} %get-tuple-element.105), channel_id=1, source_target_pairs={{0,8},{2,10},{4,12},{6,14},{8,16},{10,18},{12,20},{14,22},{16,24},... | collective-permute-start | bytes 245768 | tf_op jit(solution)/shard_map/ppermute | solution.py:520
  9.8 11.3 %collective-permute-start.6 = (bf16[64,2048]{1,0:T(8,128)(2,1)}, bf16[64,2048]{1,0:T(8,128)(2,1)S(1)}, u32[]{:S(2)}, u32[]{:S(2)}) collective-permute-start(bf16[64,2048]{1,0:T(8,128)(2,1)} %tokens.3), channel_id=1, source_target_pairs={{0,1},{1,0},{2,3},{3,2},{4,5},{5,4},{6,7},{7,6},{8,9},{9,8},{10,11... | collective-permute-start | bytes 786440 | tf_op jit(solution)/shard_map/ppermute | solution.py:534
  17.5 14.9 %collective-permute-start.5 = (bf16[256,640]{1,0:T(8,128)(2,1)S(1)}, bf16[256,640]{1,0:T(8,128)(2,1)S(1)}, u32[]{:S(2)}, u32[]{:S(2)}) collective-permute-start(bf16[256,640]{1,0:T(8,128)(2,1)S(1)} %constant_dynamic-update-slice_fusion.refs_0_.refs_3_), channel_id=1, source_target_pairs={{0,6},{2,4},{4,2},{6,0},{8,14},{10,12},{12,10},{14,8},{16,22},{18,... | collective-permute-start | bytes 983048 | tf_op jit(solution)/shard_map/ppermute | solution.py:531
  20.0 15.1 %collective-permute-start.4 = (bf16[256,640]{1,0:T(8,128)(2,1)S(1)}, bf16[256,640]{1,0:T(8,128)(2,1)S(1)}, u32[]{:S(2)}, u32[]{:S(2)}) collective-permute-start(bf16[256,640]{1,0:T(8,128)(2,1)S(1)} %constant_dynamic-update-slice_fusion.refs_0_.refs_3_), channel_id=1, source_target_pairs={{0,4},{2,6},{4,0},{6,2},{8,12},{10,14},{12,8},{14,10},{16,20},{18,... | collective-permute-start | bytes 983048 | tf_op jit(solution)/shard_map/ppermute | solution.py:531
  20.5 14.7 %collective-permute-start.3 = (bf16[256,640]{1,0:T(8,128)(2,1)S(1)}, bf16[256,640]{1,0:T(8,128)(2,1)S(1)}, u32[]{:S(2)}, u32[]{:S(2)}) collective-permute-start(bf16[256,640]{1,0:T(8,128)(2,1)S(1)} %constant_dynamic-update-slice_fusion.refs_0_.refs_3_), channel_id=1, source_target_pairs={{0,2},{2,0},{4,6},{6,4},{8,10},{10,8},{12,14},{14,12},{16,18},{18,... | collective-permute-start | bytes 983048 | tf_op jit(solution)/shard_map/ppermute | solution.py:531
  21.1 15.2 %collective-permute-start.8 = (bf16[256,640]{1,0:T(8,128)(2,1)S(1)}, bf16[256,640]{1,0:T(8,128)(2,1)S(1)}, u32[]{:S(2)}, u32[]{:S(2)}) collective-permute-start(bf16[256,640]{1,0:T(8,128)(2,1)S(1)} %constant_dynamic-update-slice_fusion.refs_0_.refs_3_), channel_id=1, source_target_pairs={{0,1},{1,0},{2,3},{3,2},{4,5},{5,4},{6,7},{7,6},{8,9},{9,8},{10,11... | collective-permute-start | bytes 983048 | tf_op jit(solution)/shard_map/ppermute | solution.py:534
  24.1 2.8 %copy-start.3 = (bf16[2048,1536]{1,0:T(8,128)(2,1)S(1)}, bf16[2048,1536]{1,0:T(8,128)(2,1)}, u32[]{:S(2)}) copy-start(bf16[2048,1536]{1,0:T(8,128)(2,1)} %q_weight.1) | copy-start | bytes 18874372
  26.9 0.8 copy-start.6
  27.7 0.8 copy-start.7
  28.6 7.2 %copy-start.1 = (bf16[1,2048,704]{1,2,0:T(8,128)(2,1)S(1)}, bf16[1,2048,704]{1,2,0:T(8,128)(2,1)}, u32[]{:S(2)}) copy-start(bf16[1,2048,704]{1,2,0:T(8,128)(2,1)} %param.26) | copy-start | bytes 8650756
  28.6 9.2 %copy-start.2 = (bf16[1,704,2048]{2,1,0:T(8,128)(2,1)S(1)}, bf16[1,704,2048]{2,1,0:T(8,128)(2,1)}, u32[]{:S(2)}) copy-start(bf16[1,704,2048]{2,1,0:T(8,128)(2,1)} %refs_6_.5) | copy-start | bytes 8650756
  28.6 9.4 %copy-start.10 = (s32[16,2]{0,1:T(2,128)S(1)}, s32[16,2]{0,1:T(2,128)}, u32[]{:S(2)}) copy-start(s32[16,2]{0,1:T(2,128)} %param.16) | copy-start | bytes 388
  28.6 9.4 %copy-start.12 = (bf16[8,512,128]{2,1,0:T(8,128)(2,1)S(1)}, bf16[8,512,128]{2,1,0:T(8,128)(2,1)}, u32[]{:S(2)}) copy-start(bf16[8,512,128]{2,1,0:T(8,128)(2,1)} %refs_11_.1) | copy-start | bytes 3145732
  35.2 1.6 %collective-permute-start.9 = (bf16[256,640]{1,0:T(8,128)(2,1)S(1)}, bf16[256,640]{1,0:T(8,128)(2,1)S(1)}, u32[]{:S(2)}, u32[]{:S(2)}) collective-permute-start(bf16[256,640]{1,0:T(8,128)(2,1)S(1)} %collective-permute-done.3.refs_4_), channel_id=1, source_target_pairs={{0,1},{1,0},{2,3},{3,2},{4,5},{5,4},{6,7},{7,6},{8,9},{9,8},{10,11... | collective-permute-start | bytes 983048 | tf_op jit(solution)/shard_map/ppermute | solution.py:534
  35.2 2.1 %collective-permute-start.10 = (bf16[256,640]{1,0:T(8,128)(2,1)S(1)}, bf16[256,640]{1,0:T(8,128)(2,1)S(1)}, u32[]{:S(2)}, u32[]{:S(2)}) collective-permute-start(bf16[256,640]{1,0:T(8,128)(2,1)S(1)} %collective-permute-done.4.refs_5_), channel_id=1, source_target_pairs={{0,1},{1,0},{2,3},{3,2},{4,5},{5,4},{6,7},{7,6},{8,9},{9,8},{10,11... | collective-permute-start | bytes 983048 | tf_op jit(solution)/shard_map/ppermute | solution.py:534
  35.7 2.1 %collective-permute-start.11 = (bf16[256,640]{1,0:T(8,128)(2,1)S(1)}, bf16[256,640]{1,0:T(8,128)(2,1)S(1)}, u32[]{:S(2)}, u32[]{:S(2)}) collective-permute-start(bf16[256,640]{1,0:T(8,128)(2,1)S(1)} %collective-permute-done.5.refs_6_), channel_id=1, source_target_pairs={{0,1},{1,0},{2,3},{3,2},{4,5},{5,4},{6,7},{7,6},{8,9},{9,8},{10,11... | collective-permute-start | bytes 983048 | tf_op jit(solution)/shard_map/ppermute | solution.py:534
  35.7 16.2 %copy-start.9 = (f32[2048]{0:T(1024)S(1)}, f32[2048]{0:T(1024)}, u32[]{:S(2)}) copy-start(f32[2048]{0:T(1024)} %param.24) | copy-start | bytes 24580
  35.7 13.5 %collective-permute-start.13 = (bf16[1,704,2048]{2,1,0:T(8,128)(2,1)S(1)}, bf16[1,704,2048]{2,1,0:T(8,128)(2,1)S(1)}, u32[]{:S(2)}, u32[]{:S(2)}) collective-permute-start(bf16[1,704,2048]{2,1,0:T(8,128)(2,1)S(1)} %bitcast.13), channel_id=1, source_target_pairs={{0,1},{1,0},{2,3},{3,2},{4,5},{5,4},{6,7},{7,6},{8,9},{9,8},{10,11... | collective-permute-start | bytes 8650760 | tf_op jit(solution)/shard_map/ppermute | solution.py:534
  37.8 12.6 %collective-permute-start.14 = (bf16[1,704,2048]{2,1,0:T(8,128)(2,1)S(1)}, bf16[1,704,2048]{2,1,0:T(8,128)(2,1)S(1)}, u32[]{:S(2)}, u32[]{:S(2)}) collective-permute-start(bf16[1,704,2048]{2,1,0:T(8,128)(2,1)S(1)} %copy-done.2), channel_id=1, source_target_pairs={{0,1},{1,0},{2,3},{3,2},{4,5},{5,4},{6,7},{7,6},{8,9},{9,8},{10,11... | collective-permute-start | bytes 8650760 | tf_op jit(solution)/shard_map/ppermute | solution.py:534
  37.9 2.2 %copy-start.11 = (bf16[1024,2048]{1,0:T(8,128)(2,1)S(1)}, bf16[1024,2048]{1,0:T(8,128)(2,1)}, u32[]{:S(2)}) copy-start(bf16[1024,2048]{1,0:T(8,128)(2,1)} %refs_12_.1) | copy-start | bytes 12582916
  40.1 33.2 %copy-start = (bf16[1,2048,704]{1,2,0:T(8,128)(2,1)S(1)}, bf16[1,2048,704]{1,2,0:T(8,128)(2,1)}, u32[]{:S(2)}) copy-start(bf16[1,2048,704]{1,2,0:T(8,128)(2,1)} %param.25) | copy-start | bytes 8650756
  48.7 1.6 %collective-permute-start.12 = (bf16[64,2048]{1,0:T(8,128)(2,1)S(1)}, bf16[64,2048]{1,0:T(8,128)(2,1)S(1)}, u32[]{:S(2)}, u32[]{:S(2)}) collective-permute-start(bf16[64,2048]{1,0:T(8,128)(2,1)S(1)} %get-tuple-element.133), channel_id=1, source_target_pairs={{0,1},{1,0},{2,3},{3,2},{4,5},{5,4},{6,7},{7,6},{8,9},{9,8},{10,11... | collective-permute-start | bytes 786440 | tf_op jit(solution)/shard_map/ppermute | solution.py:534
  49.2 24.1 %copy-start.13 = (bf16[1,704,2048]{2,1,0:T(8,128)(2,1)}, bf16[1,704,2048]{2,1,0:T(8,128)(2,1)S(1)}, u32[]{:S(2)}) copy-start(bf16[1,704,2048]{2,1,0:T(8,128)(2,1)S(1)} %collective-permute-done.13.refs_8_) | copy-start | bytes 8650756
  50.4 1.6 %copy-start.14 = (bf16[1,704,2048]{2,1,0:T(8,128)(2,1)}, bf16[1,704,2048]{2,1,0:T(8,128)(2,1)S(1)}, u32[]{:S(2)}) copy-start(bf16[1,704,2048]{2,1,0:T(8,128)(2,1)S(1)} %collective-permute-done.14.refs_9_) | copy-start | bytes 8650756
  52.2 8.6 %collective-permute-start.16 = (bf16[64,2048]{1,0:T(8,128)(2,1)S(1)}, bf16[64,2048]{1,0:T(8,128)(2,1)S(1)}, u32[]{:S(2)}, u32[]{:S(2)}) collective-permute-start(bf16[64,2048]{1,0:T(8,128)(2,1)S(1)} %get-tuple-element.141.refs_1_), channel_id=1, source_target_pairs={{0,24},{2,26},{4,28},{6,30},{8,0},{10,2},{12,4},{14,6},{16,8},{18,... | collective-permute-start | bytes 786440 | tf_op jit(solution)/shard_map/ppermute | solution.py:520
  52.5 14.5 %collective-permute-start.15 = (bf16[64,2048]{1,0:T(8,128)(2,1)S(1)}, bf16[64,2048]{1,0:T(8,128)(2,1)S(1)}, u32[]{:S(2)}, u32[]{:S(2)}) collective-permute-start(bf16[64,2048]{1,0:T(8,128)(2,1)S(1)} %get-tuple-element.141.refs_1_), channel_id=1, source_target_pairs={{0,8},{2,10},{4,12},{6,14},{8,16},{10,18},{12,20},{14,22},{16,24},... | collective-permute-start | bytes 786440 | tf_op jit(solution)/shard_map/ppermute | solution.py:520
  54.7 14.4 %collective-permute-start.17 = (bf16[36,2048]{1,0:T(8,128)(2,1)S(1)}, bf16[36,2048]{1,0:T(8,128)(2,1)S(1)}, u32[]{:S(2)}, u32[]{:S(2)}) collective-permute-start(bf16[36,2048]{1,0:T(8,128)(2,1)S(1)} %get-tuple-element.149), channel_id=1, source_target_pairs={{0,2},{2,0},{4,6},{6,4},{8,10},{10,8},{12,14},{14,12},{16,18},{18,... | collective-permute-start | bytes 442376 | tf_op jit(solution)/shard_map/ppermute | solution.py:531
  56.2 12.9 %collective-permute-start.18 = (bf16[36,2048]{1,0:T(8,128)(2,1)S(1)}, bf16[36,2048]{1,0:T(8,128)(2,1)S(1)}, u32[]{:S(2)}, u32[]{:S(2)}) collective-permute-start(bf16[36,2048]{1,0:T(8,128)(2,1)S(1)} %get-tuple-element.150), channel_id=1, source_target_pairs={{0,4},{2,6},{4,0},{6,2},{8,12},{10,14},{12,8},{14,10},{16,20},{18,... | collective-permute-start | bytes 442376 | tf_op jit(solution)/shard_map/ppermute | solution.py:531
  56.9 12.2 %collective-permute-start.19 = (bf16[36,2048]{1,0:T(8,128)(2,1)S(1)}, bf16[36,2048]{1,0:T(8,128)(2,1)S(1)}, u32[]{:S(2)}, u32[]{:S(2)}) collective-permute-start(bf16[36,2048]{1,0:T(8,128)(2,1)S(1)} %get-tuple-element.151), channel_id=1, source_target_pairs={{0,6},{2,4},{4,2},{6,0},{8,14},{10,12},{12,10},{14,8},{16,22},{18,... | collective-permute-start | bytes 442376 | tf_op jit(solution)/shard_map/ppermute | solution.py:531
  67.5 15.7 %collective-permute-start.20 = (bf16[72,2048]{1,0:T(8,128)(2,1)S(1)}, bf16[72,2048]{1,0:T(8,128)(2,1)S(1)}, u32[]{:S(2)}, u32[]{:S(2)}) collective-permute-start(bf16[72,2048]{1,0:T(8,128)(2,1)S(1)} %get-tuple-element.162), channel_id=1, source_target_pairs={{0,2},{2,0},{4,6},{6,4},{8,10},{10,8},{12,14},{14,12},{16,18},{18,... | collective-permute-start | bytes 884744 | tf_op jit(solution)/shard_map/ppermute | solution.py:531
  69.1 11.5 %collective-permute-start.23 = (bf16[64,2048]{1,0:T(8,128)(2,1)S(1)}, bf16[64,2048]{1,0:T(8,128)(2,1)S(1)}, u32[]{:S(2)}, u32[]{:S(2)}) collective-permute-start(bf16[64,2048]{1,0:T(8,128)(2,1)S(1)} %collective-permute-done.15.refs_1_), channel_id=1, source_target_pairs={{8,16},{10,18},{12,20},{14,22},{16,24},{18,26},{20,28},{22,30},{9,... | collective-permute-start | bytes 786440 | tf_op jit(solution)/shard_map/ppermute | solution.py:528
  69.8 10.8 %collective-permute-start.24 = (bf16[64,2048]{1,0:T(8,128)(2,1)S(1)}, bf16[64,2048]{1,0:T(8,128)(2,1)S(1)}, u32[]{:S(2)}, u32[]{:S(2)}) collective-permute-start(bf16[64,2048]{1,0:T(8,128)(2,1)S(1)} %collective-permute-done.16.refs_2_), channel_id=1, source_target_pairs={{8,0},{10,2},{12,4},{14,6},{16,8},{18,10},{20,12},{22,14},{9,1},{1... | collective-permute-start | bytes 786440 | tf_op jit(solution)/shard_map/ppermute | solution.py:528
  71.3 19.8 %collective-permute-start.21 = (bf16[72,2048]{1,0:T(8,128)(2,1)S(1)}, bf16[72,2048]{1,0:T(8,128)(2,1)S(1)}, u32[]{:S(2)}, u32[]{:S(2)}) collective-permute-start(bf16[72,2048]{1,0:T(8,128)(2,1)S(1)} %get-tuple-element.163), channel_id=1, source_target_pairs={{0,4},{2,6},{4,0},{6,2},{8,12},{10,14},{12,8},{14,10},{16,20},{18,... | collective-permute-start | bytes 884744 | tf_op jit(solution)/shard_map/ppermute | solution.py:531
  72.1 19.0 %collective-permute-start.22 = (bf16[72,2048]{1,0:T(8,128)(2,1)S(1)}, bf16[72,2048]{1,0:T(8,128)(2,1)S(1)}, u32[]{:S(2)}, u32[]{:S(2)}) collective-permute-start(bf16[72,2048]{1,0:T(8,128)(2,1)S(1)} %get-tuple-element.164), channel_id=1, source_target_pairs={{0,6},{2,4},{4,2},{6,0},{8,14},{10,12},{12,10},{14,8},{16,22},{18,... | collective-permute-start | bytes 884744 | tf_op jit(solution)/shard_map/ppermute | solution.py:531
  80.9 19.0 %collective-permute-start.25 = (bf16[36,2048]{1,0:T(8,128)(2,1)S(1)}, bf16[36,2048]{1,0:T(8,128)(2,1)S(1)}, u32[]{:S(2)}, u32[]{:S(2)}) collective-permute-start(bf16[36,2048]{1,0:T(8,128)(2,1)S(1)} %get-tuple-element.179), channel_id=1, source_target_pairs={{0,2},{2,0},{4,6},{6,4},{8,10},{10,8},{12,14},{14,12},{16,18},{18,... | collective-permute-start | bytes 442376 | tf_op jit(solution)/shard_map/ppermute | solution.py:531
  82.5 17.4 %collective-permute-start.26 = (bf16[36,2048]{1,0:T(8,128)(2,1)S(1)}, bf16[36,2048]{1,0:T(8,128)(2,1)S(1)}, u32[]{:S(2)}, u32[]{:S(2)}) collective-permute-start(bf16[36,2048]{1,0:T(8,128)(2,1)S(1)} %get-tuple-element.180), channel_id=1, source_target_pairs={{0,4},{2,6},{4,0},{6,2},{8,12},{10,14},{12,8},{14,10},{16,20},{18,... | collective-permute-start | bytes 442376 | tf_op jit(solution)/shard_map/ppermute | solution.py:531
  83.2 16.7 %collective-permute-start.27 = (bf16[36,2048]{1,0:T(8,128)(2,1)S(1)}, bf16[36,2048]{1,0:T(8,128)(2,1)S(1)}, u32[]{:S(2)}, u32[]{:S(2)}) collective-permute-start(bf16[36,2048]{1,0:T(8,128)(2,1)S(1)} %get-tuple-element.181), channel_id=1, source_target_pairs={{0,6},{2,4},{4,2},{6,0},{8,14},{10,12},{12,10},{14,8},{16,22},{18,... | collective-permute-start | bytes 442376 | tf_op jit(solution)/shard_map/ppermute | solution.py:531
  99.9 11.0 %collective-permute-start.28 = (bf16[72,2048]{1,0:T(8,128)(2,1)S(1)}, bf16[72,2048]{1,0:T(8,128)(2,1)S(1)}, u32[]{:S(2)}, u32[]{:S(2)}) collective-permute-start(bf16[72,2048]{1,0:T(8,128)(2,1)S(1)} %get-tuple-element.183), channel_id=1, source_target_pairs={{0,2},{2,0},{4,6},{6,4},{8,10},{10,8},{12,14},{14,12},{16,18},{18,... | collective-permute-start | bytes 884744 | tf_op jit(solution)/shard_map/ppermute | solution.py:531
  100.5 10.4 %collective-permute-start.29 = (bf16[72,2048]{1,0:T(8,128)(2,1)S(1)}, bf16[72,2048]{1,0:T(8,128)(2,1)S(1)}, u32[]{:S(2)}, u32[]{:S(2)}) collective-permute-start(bf16[72,2048]{1,0:T(8,128)(2,1)S(1)} %get-tuple-element.184), channel_id=1, source_target_pairs={{0,4},{2,6},{4,0},{6,2},{8,12},{10,14},{12,8},{14,10},{16,20},{18,... | collective-permute-start | bytes 884744 | tf_op jit(solution)/shard_map/ppermute | solution.py:531
  102.0 9.0 %collective-permute-start.30 = (bf16[72,2048]{1,0:T(8,128)(2,1)S(1)}, bf16[72,2048]{1,0:T(8,128)(2,1)S(1)}, u32[]{:S(2)}, u32[]{:S(2)}) collective-permute-start(bf16[72,2048]{1,0:T(8,128)(2,1)S(1)} %get-tuple-element.185), channel_id=1, source_target_pairs={{0,6},{2,4},{4,2},{6,0},{8,14},{10,12},{12,10},{14,8},{16,22},{18,... | collective-permute-start | bytes 884744 | tf_op jit(solution)/shard_map/ppermute | solution.py:531
  111.7 18.3 %collective-permute-start.34 = (bf16[64,2048]{1,0:T(8,128)(2,1)S(1)}, bf16[64,2048]{1,0:T(8,128)(2,1)S(1)}, u32[]{:S(2)}, u32[]{:S(2)}) collective-permute-start(bf16[64,2048]{1,0:T(8,128)(2,1)S(1)} %get-tuple-element.197), channel_id=1, source_target_pairs={{0,24},{2,26},{4,28},{6,30},{8,0},{10,2},{12,4},{14,6},{16,8},{18,... | collective-permute-start | bytes 786440 | tf_op jit(solution)/shard_map/ppermute | solution.py:520
  113.2 16.8 %collective-permute-start.35 = (bf16[64,2048]{1,0:T(8,128)(2,1)S(1)}, bf16[64,2048]{1,0:T(8,128)(2,1)S(1)}, u32[]{:S(2)}, u32[]{:S(2)}) collective-permute-start(bf16[64,2048]{1,0:T(8,128)(2,1)S(1)} %get-tuple-element.198), channel_id=1, source_target_pairs={{0,8},{2,10},{4,12},{6,14},{8,16},{10,18},{12,20},{14,22},{16,24},... | collective-permute-start | bytes 786440 | tf_op jit(solution)/shard_map/ppermute | solution.py:520
  115.4 5.3 %collective-permute-start.31 = (bf16[36,2048]{1,0:T(8,128)(2,1)S(1)}, bf16[36,2048]{1,0:T(8,128)(2,1)S(1)}, u32[]{:S(2)}, u32[]{:S(2)}) collective-permute-start(bf16[36,2048]{1,0:T(8,128)(2,1)S(1)} %get-tuple-element.191), channel_id=1, source_target_pairs={{0,2},{2,0},{4,6},{6,4},{8,10},{10,8},{12,14},{14,12},{16,18},{18,... | collective-permute-start | bytes 442376 | tf_op jit(solution)/shard_map/ppermute | solution.py:531
  116.4 5.5 %collective-permute-start.32 = (bf16[36,2048]{1,0:T(8,128)(2,1)S(1)}, bf16[36,2048]{1,0:T(8,128)(2,1)S(1)}, u32[]{:S(2)}, u32[]{:S(2)}) collective-permute-start(bf16[36,2048]{1,0:T(8,128)(2,1)S(1)} %get-tuple-element.192), channel_id=1, source_target_pairs={{0,4},{2,6},{4,0},{6,2},{8,12},{10,14},{12,8},{14,10},{16,20},{18,... | collective-permute-start | bytes 442376 | tf_op jit(solution)/shard_map/ppermute | solution.py:531
  117.1 7.9 %collective-permute-start.33 = (bf16[36,2048]{1,0:T(8,128)(2,1)S(1)}, bf16[36,2048]{1,0:T(8,128)(2,1)S(1)}, u32[]{:S(2)}, u32[]{:S(2)}) collective-permute-start(bf16[36,2048]{1,0:T(8,128)(2,1)S(1)} %get-tuple-element.193), channel_id=1, source_target_pairs={{0,6},{2,4},{4,2},{6,0},{8,14},{10,12},{12,10},{14,8},{16,22},{18,... | collective-permute-start | bytes 442376 | tf_op jit(solution)/shard_map/ppermute | solution.py:531
  125.5 13.1 %collective-permute-start.39 = (bf16[64,2048]{1,0:T(8,128)(2,1)S(1)}, bf16[64,2048]{1,0:T(8,128)(2,1)S(1)}, u32[]{:S(2)}, u32[]{:S(2)}) collective-permute-start(bf16[64,2048]{1,0:T(8,128)(2,1)S(1)} %unpack_rows.4), channel_id=1, source_target_pairs={{0,16},{2,18},{4,20},{6,22},{8,24},{10,26},{12,28},{14,30},{16,0},... | collective-permute-start | bytes 786440 | tf_op jit(solution)/shard_map/ppermute | solution.py:520
  130.0 5.3 %collective-permute-start.36 = (bf16[36,2048]{1,0:T(8,128)(2,1)S(1)}, bf16[36,2048]{1,0:T(8,128)(2,1)S(1)}, u32[]{:S(2)}, u32[]{:S(2)}) collective-permute-start(bf16[36,2048]{1,0:T(8,128)(2,1)S(1)} %get-tuple-element.202), channel_id=1, source_target_pairs={{0,2},{2,0},{4,6},{6,4},{8,10},{10,8},{12,14},{14,12},{16,18},{18,... | collective-permute-start | bytes 442376 | tf_op jit(solution)/shard_map/ppermute | solution.py:531
  130.8 5.3 %collective-permute-start.37 = (bf16[36,2048]{1,0:T(8,128)(2,1)S(1)}, bf16[36,2048]{1,0:T(8,128)(2,1)S(1)}, u32[]{:S(2)}, u32[]{:S(2)}) collective-permute-start(bf16[36,2048]{1,0:T(8,128)(2,1)S(1)} %get-tuple-element.203), channel_id=1, source_target_pairs={{0,4},{2,6},{4,0},{6,2},{8,12},{10,14},{12,8},{14,10},{16,20},{18,... | collective-permute-start | bytes 442376 | tf_op jit(solution)/shard_map/ppermute | solution.py:531
  131.9 6.2 %collective-permute-start.38 = (bf16[36,2048]{1,0:T(8,128)(2,1)S(1)}, bf16[36,2048]{1,0:T(8,128)(2,1)S(1)}, u32[]{:S(2)}, u32[]{:S(2)}) collective-permute-start(bf16[36,2048]{1,0:T(8,128)(2,1)S(1)} %get-tuple-element.204), channel_id=1, source_target_pairs={{0,6},{2,4},{4,2},{6,0},{8,14},{10,12},{12,10},{14,8},{16,22},{18,... | collective-permute-start | bytes 442376 | tf_op jit(solution)/shard_map/ppermute | solution.py:531
